TPU v7x, 256 devices: a whole 4x4x8 slice. The times are simulated.
256 devices in a mesh: gz: 32 (over x_lo, z, core), box: 8 (over x_hi, y).
Axes of the slice: x: 4 (x_hi: 2, x_lo: 2; x = x_hi * 2 + x_lo), y: 4, z: 8, core: 2. Of those that a mesh axis runs over, the one named last changes fastest.
Arguments:
- sources: float32 [512, 16, 16, 1024], P('gz', 'box'), may hold values from -6 to 6
- leaf_maps: float32 [32, 16, 1024, 1024], P('gz', 'box'), may hold values from -1 to 1, as said below
- mode_ids: int32 [32], replicated, may hold values from 0 to 511, as said below
Outputs:
- merged_map: float32 [32, 8, 512, 1024], P('gz', 'box')
- merged_data: float32 [32, 8, 16, 512], P('gz', 'box')
Inputs may be any that keep to these rules, and one draw needn't show every extreme that they name: `mode_ids`: distinct mode numbers; 0 and 511 are always among them. `leaf_maps`: every leaf map is a contraction: its operator norm is below 1.
All inputs are finite; a program needn't handle non-finite values.
Results may differ from a plain program's by a relative error of at most 0.000082.
Values sent between devices are 32-bit elements; how exact they have to be, the bound alone decides.
A program may use at most 128 MiB of HBM per device.

v0:
```python
import jax
import jax.numpy as jnp
from jax import lax
from jax.sharding import PartitionSpec as P

NZ = 512


def swapped(block, axis, apart):
    count = lax.axis_size(axis)
    route = []
    for low in range(count):
        high = low | 1 << apart
        if high != low and high < count:
            route += [(low, high), (high, low)]
    return lax.ppermute(block, axis, route)


def hard_dot(left_mat, right_mat):
    return jnp.dot(
        left_mat, right_mat, precision=lax.Precision.HIGHEST, preferred_element_type=jnp.float32
    )


def cas_table(mode_list, z_index, length_z):
    phase = mode_list[:, None] * z_index[None, :] % length_z
    angle = phase.astype(jnp.float32) * (2.0 * jnp.pi / length_z)
    return (jnp.cos(angle) + jnp.sin(angle)) / jnp.sqrt(jnp.float32(length_z))


def solve_face(a_31, a_33, b_33, b_32, h_3, g_3):
    face = a_33.shape[0]
    system = jnp.eye(face, dtype=jnp.float32) - hard_dot(a_33, b_33)
    wanted = jnp.concatenate([a_31, -hard_dot(a_33, b_32), (h_3 - hard_dot(g_3, a_33.T)).T], axis=1)
    factor = jnp.linalg.cholesky(hard_dot(system.T, system))
    middle = lax.linalg.triangular_solve(
        factor, hard_dot(system.T, wanted), left_side=True, lower=True
    )
    solved = lax.linalg.triangular_solve(
        factor, middle, left_side=True, lower=True, transpose_a=True
    )
    return (solved[:, :face], solved[:, face : 2 * face], solved[:, 2 * face :])


def left_rows(a_11, a_13, b_33, b_32, h_1, g_3, x_one, x_two, x_data):
    top_left = a_11 + hard_dot(a_13, hard_dot(b_33, x_one))
    top_right = hard_dot(a_13, hard_dot(b_33, x_two) - b_32)
    data_left = h_1 + hard_dot(a_13, hard_dot(b_33, x_data) - g_3.T).T
    return (jnp.concatenate([top_left, top_right], axis=1), data_left)


def right_rows(b_23, b_22, g_2, x_one, x_two, x_data):
    low_left = -hard_dot(b_23, x_one)
    low_right = b_22 - hard_dot(b_23, x_two)
    data_right = g_2 - hard_dot(b_23, x_data).T
    return (jnp.concatenate([low_left, low_right], axis=1), data_right)


def merge_full(a_map, b_map, a_data, b_data):
    face = a_map.shape[0] // 2
    x_one, x_two, x_data = solve_face(
        a_map[face:, :face],
        a_map[face:, face:],
        b_map[:face, :face],
        b_map[:face, face:],
        a_data[:, face:],
        b_data[:, :face],
    )
    top_rows, data_left = left_rows(
        a_map[:face, :face],
        a_map[:face, face:],
        b_map[:face, :face],
        b_map[:face, face:],
        a_data[:, :face],
        b_data[:, :face],
        x_one,
        x_two,
        x_data,
    )
    low_rows, data_right = right_rows(
        b_map[face:, :face], b_map[face:, face:], b_data[:, face:], x_one, x_two, x_data
    )
    return (
        jnp.concatenate([top_rows, low_rows], axis=0),
        jnp.concatenate([data_left, data_right], axis=1),
    )


def local(sources, leaf_maps, mode_ids):
    slab_planes = sources.shape[0]
    points = leaf_maps.shape[-1]
    face = points // 2
    z_index = lax.axis_index("gz") * slab_planes + jnp.arange(slab_planes, dtype=jnp.int32)
    cas_rows = cas_table(mode_ids, z_index, NZ)
    spectral = lax.psum_scatter(
        jnp.einsum("mz,zbrp->mbrp", cas_rows, sources, precision=lax.Precision.HIGHEST),
        "gz",
        scatter_dimension=0,
        tiled=True,
    )
    mode_slot = 0
    one_map, one_data = merge_full(
        leaf_maps[mode_slot, 0],
        leaf_maps[mode_slot, 1],
        spectral[mode_slot, 0],
        spectral[mode_slot, 1],
    )
    level_maps = [one_map]
    level_data = [one_data]
    merged = jnp.stack(level_maps)
    merged_info = jnp.stack(level_data)
    is_left = lax.axis_index("box") % 2 == 0
    other_map, other_data = swapped((merged, merged_info), "box", 0)
    a_whole = jnp.where(is_left, merged, other_map)
    b_whole = jnp.where(is_left, other_map, merged)
    a_info = jnp.where(is_left, merged_info, other_data)
    b_info = jnp.where(is_left, other_data, merged_info)
    a_top = a_whole[:, :face]
    a_bottom = a_whole[:, face:]
    b_top = b_whole[:, :face]
    b_bottom = b_whole[:, face:]
    h_one = a_info[:, :, :face]
    h_three = a_info[:, :, face:]
    g_three = b_info[:, :, :face]
    g_two = b_info[:, :, face:]
    mode_slot = 0
    a_31 = a_bottom[mode_slot][:, :face]
    a_33 = a_bottom[mode_slot][:, face:]
    b_33 = b_top[mode_slot][:, :face]
    b_32 = b_top[mode_slot][:, face:]
    x_one, x_two, x_data = solve_face(
        a_31, a_33, b_33, b_32, h_three[mode_slot], g_three[mode_slot]
    )

    def take_left(slot=mode_slot, first=x_one, second=x_two, third=x_data):
        return left_rows(
            a_top[slot][:, :face],
            a_top[slot][:, face:],
            b_top[slot][:, :face],
            b_top[slot][:, face:],
            h_one[slot],
            g_three[slot],
            first,
            second,
            third,
        )

    def take_right(slot=mode_slot, first=x_one, second=x_two, third=x_data):
        return right_rows(
            b_bottom[slot][:, :face], b_bottom[slot][:, face:], g_two[slot], first, second, third
        )

    map_half, data_half = lax.cond(is_left, take_left, take_right)
    out_maps = [map_half * jnp.sqrt(jnp.float32(points))]
    out_data = [data_half]
    merged_map = jnp.stack(out_maps)[:, None]
    merged_data = jnp.stack(out_data)[:, None]
    return (merged_map, merged_data)


def solution(mesh):
    placed = (P("gz", "box", None, None), P("gz", "box", None, None), P())
    return jax.shard_map(
        local,
        mesh=mesh,
        in_specs=placed,
        out_specs=(P("gz", "box", None, None), P("gz", "box", None, None)),
        check_vma=False,
    )
```

profile of v0, /device:TPU:20, one launch (start us, length us, event | category | flops | bytes accessed | tf_op | source)
XLA Modules:
  0.0 524.4 jit_solution(850306666708887465)
XLA Ops:
  7.2 1.5 copy-done
  8.8 5.0 fusion.25
  13.8 4.4 copy.21
  18.2 8.3 %fusion.188 = (f32[1,1,1024,1024]{3,2,1,0:T(8,128)}, f32[1,1,1024,1024]{3,2,1,0:T(8,128)}) fusion(f32[1,2,1024,1024]{3,2,1,0:T(8,128)} %param.11), kind=kLoop, calls=%fused_computation.303 | loop fusion | bytes 16777216 | tf_op jit(solution)/shard_map/slice | solution.py:103
  26.5 5.4 %copy.36 = f32[1,1,1024,1024]{2,3,1,0:T(8,128)} copy(f32[1,1,1024,1024]{3,2,1,0:T(8,128)} %get-tuple-element.129) | data formatting | bytes 8388608
  31.9 2.3 slice.383
  34.2 5.5 %copy.37 = f32[1,1,1024,1024]{2,3,1,0:T(8,128)} copy(f32[1,1,1024,1024]{3,2,1,0:T(8,128)} %get-tuple-element.130) | data formatting | bytes 8388608
  39.7 5.0 convert_subtract_fusion.1
  44.7 1.9 fusion.191
  48.2 11.7 %cholesky.286 = f32[128,128]{1,0:T(8,128)S(1)} custom-call(f32[128,128]{1,0:T(8,128)S(1)} %cholesky.426), custom_call_target="Cholesky" | custom-call | tf_op jit(solution)/shard_map/jit(cholesky)/cholesky | solution.py:35
  59.9 9.8 %custom-call.31 = f32[1,128,128]{1,2,0:T(8,128)S(1)} custom-call(f32[1,128,128]{2,1,0:T(8,128)S(1)} %get-tuple-element.158), custom_call_target="InvertDiagBlocksLowerTriangular" | custom-call | tf_op jit(solution)/shard_map/jit(cholesky)/cholesky | solution.py:35
  72.6 11.7 %cholesky.305 = f32[128,128]{1,0:T(8,128)S(1)} custom-call(f32[128,128]{1,0:T(8,128)S(1)} %cholesky.430), custom_call_target="Cholesky" | custom-call | tf_op jit(solution)/shard_map/jit(cholesky)/cholesky | solution.py:35
  84.3 9.8 %custom-call.32 = f32[1,128,128]{1,2,0:T(8,128)S(1)} custom-call(f32[1,128,128]{2,1,0:T(8,128)S(1)} %get-tuple-element.155), custom_call_target="InvertDiagBlocksLowerTriangular" | custom-call | tf_op jit(solution)/shard_map/jit(cholesky)/cholesky | solution.py:35
  95.7 11.7 %cholesky.326 = f32[128,128]{1,0:T(8,128)S(1)} custom-call(f32[128,128]{1,0:T(8,128)S(1)} %cholesky.435), custom_call_target="Cholesky" | custom-call | tf_op jit(solution)/shard_map/jit(cholesky)/cholesky | solution.py:35
  107.5 10.2 %custom-call.33 = f32[1,128,128]{1,2,0:T(8,128)S(1)} custom-call(f32[1,128,128]{2,1,0:T(8,128)S(1)} %get-tuple-element.152), custom_call_target="InvertDiagBlocksLowerTriangular" | custom-call | tf_op jit(solution)/shard_map/jit(cholesky)/cholesky | solution.py:35
  119.1 11.7 %cholesky.343 = f32[128,128]{1,0:T(8,128)S(1)} custom-call(f32[128,128]{1,0:T(8,128)S(1)} %convolution_subtract_fusion.21), custom_call_target="Cholesky" | custom-call | tf_op jit(solution)/shard_map/jit(cholesky)/cholesky | solution.py:35
  135.7 8.3 %while.8 = (s32[]{:T(128)}, f32[512,512]{1,0:T(8,128)S(1)}, s32[4,2]{0,1:T(2,128)S(1)}, f32[4,128,128]{2,1,0:T(8,128)S(1)}, s32[]{:T(128)}) while((s32[]{:T(128)}, f32[512,512]{1,0:T(8,128)S(1)}, s32[4,2]{0,1:T(2,128)S(1)}, f32[4,128,128]{2,1,0:T(8,128)S(1)}, s32[]{:T(128)}) %tuple.87), condition=%wide.while_cond.1, body=%wide.while_body.1.sunk | while | flops 2 | bytes 131189 | solution.py:39
  144.1 39.5 %custom-call.35 = f32[4,128,128]{1,2,0:T(8,128)S(1)} custom-call(f32[4,128,128]{2,1,0:T(8,128)S(1)} %get-tuple-element.79), custom_call_target="InvertDiagBlocksLowerTriangular" | custom-call | tf_op jit(solution)/shard_map/triangular_solve/custom-call.8 | solution.py:39
  183.6 3.4 convolution_negate_fusion.3
  188.0 1.8 fusion.51
  189.9 3.6 fusion.13
  196.8 1.5 convolution_subtract_fusion.15
  202.7 1.6 convolution_subtract_fusion.14
  205.1 2.0 copy-done.2
  207.1 1.8 fusion.48
  209.0 1.9 fusion.47
  210.8 1.9 fusion.49
  212.7 2.0 fusion.71
  214.8 1.9 fusion.50
  216.6 1.9 convolution_bitcast_fusion.3
  218.5 2.5 maximum_bitcast_fusion
  225.0 90.0 %collective-permute-done.1 = f32[1,16,1024]{2,1,0:T(8,128)S(1)} collective-permute-done((f32[1,16,1024]{2,1,0:T(8,128)S(1)}, f32[1,16,1024]{2,1,0:T(8,128)S(1)}, u32[]{:S(2)}, u32[]{:S(2)}) %collective-permute-start.1) | collective-permute-done | bytes 65568 | tf_op jit(solution)/shard_map/ppermute | solution.py:16
  315.0 4.2 broadcast_select_fusion
  319.5 1.7 copy-done.5
  321.2 2.3 fusion.189
  323.4 3.5 convert_subtract_fusion
  326.9 2.9 convolution_negate_fusion.1
  330.5 1.9 fusion.192
  333.9 12.1 %cholesky.358 = f32[128,128]{1,0:T(8,128)S(1)} custom-call(f32[128,128]{1,0:T(8,128)S(1)} %cholesky.439), custom_call_target="Cholesky" | custom-call | tf_op jit(solution)/shard_map/jit(cholesky)/cholesky | solution.py:35
  346.7 9.8 %custom-call.36 = f32[1,128,128]{1,2,0:T(8,128)S(1)} custom-call(f32[1,128,128]{2,1,0:T(8,128)S(1)} %get-tuple-element.148), custom_call_target="InvertDiagBlocksLowerTriangular" | custom-call | tf_op jit(solution)/shard_map/jit(cholesky)/cholesky | solution.py:35
  359.2 11.7 %cholesky.377 = f32[128,128]{1,0:T(8,128)S(1)} custom-call(f32[128,128]{1,0:T(8,128)S(1)} %cholesky.443), custom_call_target="Cholesky" | custom-call | tf_op jit(solution)/shard_map/jit(cholesky)/cholesky | solution.py:35
  371.6 9.8 %custom-call.37 = f32[1,128,128]{1,2,0:T(8,128)S(1)} custom-call(f32[1,128,128]{2,1,0:T(8,128)S(1)} %get-tuple-element.145), custom_call_target="InvertDiagBlocksLowerTriangular" | custom-call | tf_op jit(solution)/shard_map/jit(cholesky)/cholesky | solution.py:35
  383.0 12.5 %cholesky.398 = f32[128,128]{1,0:T(8,128)} custom-call(f32[128,128]{1,0:T(8,128)S(1)} %cholesky.448), custom_call_target="Cholesky" | custom-call | tf_op jit(solution)/shard_map/jit(cholesky)/cholesky | solution.py:35
  397.0 10.4 %custom-call.38 = f32[1,128,128]{1,2,0:T(8,128)} custom-call(f32[1,128,128]{2,1,0:T(8,128)S(1)} %get-tuple-element.142), custom_call_target="InvertDiagBlocksLowerTriangular" | custom-call | tf_op jit(solution)/shard_map/jit(cholesky)/cholesky | solution.py:35
  409.7 11.7 %cholesky.415 = f32[128,128]{1,0:T(8,128)S(1)} custom-call(f32[128,128]{1,0:T(8,128)S(1)} %convolution_subtract_fusion.20), custom_call_target="Cholesky" | custom-call | tf_op jit(solution)/shard_map/jit(cholesky)/cholesky | solution.py:35
  425.7 11.9 %while.9 = (s32[]{:T(128)}, f32[512,512]{1,0:T(8,128)}, s32[4,2]{0,1:T(2,128)S(1)}, f32[4,128,128]{2,1,0:T(8,128)S(1)}, s32[]{:T(128)}) while((s32[]{:T(128)}, f32[512,512]{1,0:T(8,128)}, s32[4,2]{0,1:T(2,128)S(1)}, f32[4,128,128]{2,1,0:T(8,128)S(1)}, s32[]{:T(128)}) %tuple.99), condition=%wide.while_cond.1.clone, body=%wide.while_body.1.clone.sunk | while | flops 2 | bytes 131189 | solution.py:39
  426.4 2.3 bitcast_dynamic-update-slice_fusion.5
  429.4 2.3 bitcast_dynamic-update-slice_fusion.5
  432.4 2.3 bitcast_dynamic-update-slice_fusion.5
  435.4 2.2 bitcast_dynamic-update-slice_fusion.5
  437.6 39.7 %custom-call.40 = f32[4,128,128]{1,2,0:T(8,128)S(1)} custom-call(f32[4,128,128]{2,1,0:T(8,128)S(1)} %get-tuple-element.81), custom_call_target="InvertDiagBlocksLowerTriangular" | custom-call | tf_op jit(solution)/shard_map/triangular_solve/custom-call.8 | solution.py:39
  477.4 4.9 fusion.19
  485.6 1.5 convolution_subtract_fusion.13
  493.8 2.0 copy-done.6
  495.8 18.2 %conditional.1 = (f32[1,1,16,512]{3,2,1,0:T(8,128)S(1)}, f32[512,1024]{1,0:T(8,128)}) conditional(s32[]{:T(128)} %convert_element_type.12, (f32[1,1024,1024]{1,2,0:T(8,128)S(1)}, f32[512,512]{0,1:T(8,128)S(1)}, f32[512,512]{0,1:T(8,128)S(1)}, f32[1,16,1024]{2,1,0:T(8,128)S(1)}, f32[512,16]{0,1:T(8,128)S(1)}) %tuple.97, ...), branch_computations={%region_9.13_spmd, %region_10.14_spmd} | conditional | flops 6544179200 | bytes 50528356 | solution.py:153
  496.8 1.8 slice_bitcast_fusion.1
  498.6 2.9 copy.25
  501.5 2.4 convolution_subtract_fusion.3
  504.5 1.9 convolution_subtract_fusion.2
  506.4 1.9 fusion.11
  508.3 1.8 fusion.4
  510.1 1.9 convolution_bitcast_fusion
  512.1 1.9 copy.35
  514.0 3.4 multiply_bitcast_fusion
  (153 shorter events, 59.5 us)
Async XLA Ops:
  7.2 1.6 copy-start
  7.2 179.9 %reduce-scatter.2.cloned.1.call-start = ((), (), s32[]{:S(2)}) async-start(), calls=%async_computation.1 | async-start | bytes 4325376 | tf_op jit(solution)/shard_map/reduce_scatter | solution.py:95
  47.1 1.0 copy-start.19
  187.1 2.8 copy-start.17
  204.9 2.2 copy-start.2
  210.8 7.7 %copy-start.11 = (f32[512,512]{0,1:T(8,128)}, f32[512,512]{0,1:T(8,128)S(1)}, u32[]{:S(2)}) copy-start(f32[512,512]{0,1:T(8,128)S(1)} %fusion.47) | copy-start | bytes 3145732
  210.8 3.9 copy-start.3
  216.6 4.4 copy-start.13
  218.5 2.5 copy-start.15
  221.0 94.0 %collective-permute-start = (f32[1,1024,1024]{1,2,0:T(8,128)}, f32[1,1024,1024]{1,2,0:T(8,128)}, u32[]{:S(2)}, u32[]{:S(2)}) collective-permute-start(f32[1,1024,1024]{1,2,0:T(8,128)} %maximum_bitcast_fusion), channel_id=1, source_target_pairs={{0,1},{1,0},{2,3},{3,2},{4,5},{5,4},{6,7},{7,6},{8,9},{9,8},{10,11... | collective-permute-start | bytes 12582920 | tf_op jit(solution)/shard_map/ppermute | solution.py:16
  222.3 92.7 %copy-start.12 = (f32[512,512]{0,1:T(8,128)S(1)}, f32[512,512]{0,1:T(8,128)}, u32[]{:S(2)}) copy-start(f32[512,512]{0,1:T(8,128)} %copy-done.11) | copy-start | bytes 3145732
  222.3 92.8 %copy-start.14 = (f32[512,512]{0,1:T(8,128)S(1)}, f32[512,512]{0,1:T(8,128)}, u32[]{:S(2)}) copy-start(f32[512,512]{0,1:T(8,128)} %copy-done.13) | copy-start | bytes 3145732
  224.1 90.8 %collective-permute-start.1 = (f32[1,16,1024]{2,1,0:T(8,128)S(1)}, f32[1,16,1024]{2,1,0:T(8,128)S(1)}, u32[]{:S(2)}, u32[]{:S(2)}) collective-permute-start(f32[1,16,1024]{2,1,0:T(8,128)S(1)} %maximum_bitcast_fusion.1), channel_id=1, source_target_pairs={{0,1},{1,0},{2,3},{3,2},{4,5},{5,4},{6,7},{7,6},{8,9},{9,8},{10,11... | collective-permute-start | bytes 196616 | tf_op jit(solution)/shard_map/ppermute | solution.py:16
  319.2 2.0 copy-start.5
  319.2 7.7 %copy-start.7 = (f32[1,1024,1024]{1,2,0:T(8,128)}, f32[1,1024,1024]{1,2,0:T(8,128)S(1)}, u32[]{:S(2)}) copy-start(f32[1,1024,1024]{1,2,0:T(8,128)S(1)} %get-tuple-element.127) | copy-start | bytes 12582916
  319.5 10.4 %copy-start.4 = (f32[512,1024]{0,1:T(8,128)}, f32[512,1024]{0,1:T(8,128)S(1)}, u32[]{:S(2)}) copy-start(f32[512,1024]{0,1:T(8,128)S(1)} %slice_bitcast_fusion.2) | copy-start | bytes 6291460
  332.9 1.0 copy-start.18
  383.0 94.4 %slice-start = ((f32[512,1024]{0,1:T(8,128)}), f32[512,512]{0,1:T(8,128)S(1)}, s32[]{:S(2)}) async-start(f32[512,1024]{0,1:T(8,128)} %copy-done.4), calls=%async_computation.2 | async-start | bytes 2097152 | tf_op jit(solution)/shard_map/slice | solution.py:127
  477.4 5.5 %copy-start.16 = (f32[512,512]{1,0:T(8,128)S(1)}, f32[512,512]{1,0:T(8,128)}, u32[]{:S(2)}) copy-start(f32[512,512]{1,0:T(8,128)} %get-tuple-element.261) | copy-start | bytes 3145732
  493.6 2.2 copy-start.6
  495.8 1.0 copy-start.9
  501.5 3.0 copy-start.8
  503.9 2.5 copy-start.10
  514.0 3.4 copy-start.20
  514.0 3.4 copy-start.1
Sparse Core Ops, SparseCore 0:
  18.3 125.3 reduce-scatter.1
where the time goes:
time: 532 us; the launch traced here: 524 us
  other arithmetic  252 us (47%)
  matrix products  92.4 us (17%)
  waiting for transfers between devices  90.1 us (17%)
  local copies, waits for them, and re-layouts  67.4 us (13%)
  between operations  20.2 us (4%)
    another operation x29, other arithmetic, solve_face(): factor = jnp.linalg.cholesky(hard_dot(system.T, system))  161 us
    ppermute x2, waiting for transfers between devices, swapped(): return lax.ppermute(block, axis, route)  90 us
    another operation x7, other arithmetic, solve_face(): lax.linalg.triangular_solve(factor, middle, left_side=True, lower=True, t...  80.8 us
    dot_general x25, matrix products, hard_dot(): jnp.dot(left_mat, right_mat, precision=lax.Precision.HIGHEST, preferred_e...  53 us
    unnamed x38, local copies, waits for them, and re-layouts  20.1 us
    another operation x27, local copies, waits for them, and re-layouts, solve_face(): lax.linalg.triangular_solve(factor, middle, left_side=True, lower=True, t...  20.1 us
    another operation x12, matrix products, solve_face(): factor = jnp.linalg.cholesky(hard_dot(system.T, system))  12 us
    another operation x14, matrix products, solve_face(): lax.linalg.triangular_solve(factor, middle, left_side=True, lower=True, t...  11.6 us
  transfers between devices with their start and end apart: 3, of which 1 were waited for; matrix products, arithmetic and copies ran while one was open for 32% of the time, Pallas kernels for 0%

commit v1 on v0

v1 whole, which is shorter than its diff:
```python
import jax
import jax.numpy as jnp
from jax import lax
from jax.sharding import PartitionSpec as P

NZ = 512


def swapped(block, axis):
    count = lax.axis_size(axis)
    route = []
    for low in range(0, count, 2):
        route += [(low, low + 1), (low + 1, low)]
    return lax.ppermute(block, axis, route)


def mul(left_mat, right_mat):
    return jnp.dot(
        left_mat, right_mat, precision=lax.Precision.HIGH, preferred_element_type=jnp.float32
    )


def mul_rows(rows, mat):
    return lax.dot_general(
        rows,
        mat,
        (((1,), (1,)), ((), ())),
        precision=lax.Precision.HIGH,
        preferred_element_type=jnp.float32,
    )


def cas_table(mode_list, z_index, length_z):
    phase = mode_list[:, None] * z_index[None, :] % length_z
    angle = phase.astype(jnp.float32) * (2.0 * jnp.pi / length_z)
    return (jnp.cos(angle) + jnp.sin(angle)) / jnp.sqrt(jnp.float32(length_z))


def inverse(kernel_map):
    face = kernel_map.shape[0]
    power = mul(kernel_map, kernel_map)
    total = jnp.eye(face, dtype=jnp.float32) + kernel_map

    def again(state):
        return (state[3] > 1e-15) & (state[0] < 64)

    def step(state):
        count, total, power, _ = state
        both = mul(jnp.concatenate([total, power], axis=0), power)
        total = total + both[:face]
        power = both[face:]
        return count + 1, total, power, jnp.sum(power * power)

    state = lax.while_loop(again, step, (0, total, power, jnp.sum(power * power)))
    return state[1]


def local(sources, leaf_maps, mode_ids):
    slab_planes = sources.shape[0]
    points = leaf_maps.shape[-1]
    face = points // 2
    z_index = lax.axis_index("gz") * slab_planes + jnp.arange(slab_planes, dtype=jnp.int32)
    cas_rows = cas_table(mode_ids, z_index, NZ)
    spectral = lax.psum_scatter(
        jnp.einsum("mz,zbrp->mbrp", cas_rows, sources, precision=lax.Precision.HIGH),
        "gz",
        scatter_dimension=0,
        tiled=True,
    )
    far = lax.axis_index("box") % 2
    near = 1 - far

    def block(leaf, row, col):
        return lax.dynamic_slice(
            leaf_maps, (0, leaf, row * face, col * face), (1, 1, face, face)
        ).reshape(face, face)

    def info(leaf, side):
        rows = spectral.shape[2]
        return lax.dynamic_slice(
            spectral, (0, leaf, 0, side * face), (1, 1, rows, face)
        ).reshape(rows, face)

    a_11, a_13 = block(far, far, far), block(far, far, near)
    a_31, a_33 = block(far, near, far), block(far, near, near)
    b_33, b_32 = block(near, far, far), block(near, far, near)
    b_23, b_22 = block(near, near, far), block(near, near, near)
    inv_one = inverse(mul(a_33, b_33))
    through = mul(a_33, b_32)
    near_gain = mul(b_23, inv_one)
    o_33 = b_22 + mul(near_gain, through)
    y_33 = swapped(o_33, "box")
    o_31 = -mul(near_gain, a_31)
    y_32 = swapped(o_31, "box")
    far_gain = mul(mul(a_13, b_33), inv_one)
    o_11 = a_11 + mul(far_gain, a_31)
    o_13 = -mul(a_13, b_32) - mul(far_gain, through)
    h_1, h_3 = info(far, far), info(far, near)
    g_3, g_2 = info(near, far), info(near, near)
    jump = h_3 - mul_rows(g_3, a_33)
    near_data = g_2 - mul_rows(jump, near_gain)
    far_data = h_1 + mul_rows(jump, far_gain) - mul_rows(g_3, a_13)
    other_data = swapped(near_data, "box")
    inv_two = inverse(mul(y_33, o_33))
    gain = mul(o_13, inv_two)
    own = o_11 + mul(gain, mul(y_33, o_31))
    data = far_data + mul_rows(mul_rows(near_data, y_33) - other_data, gain)
    other = -mul(gain, y_32)
    scale = jnp.sqrt(jnp.float32(points))
    is_left = far == 0
    out = jnp.concatenate(
        [jnp.where(is_left, own, other), jnp.where(is_left, other, own)], axis=1
    )
    return ((out * scale)[None, None], data[None, None])


def solution(mesh):
    placed = (P("gz", "box", None, None), P("gz", "box", None, None), P())
    return jax.shard_map(
        local,
        mesh=mesh,
        in_specs=placed,
        out_specs=(P("gz", "box", None, None), P("gz", "box", None, None)),
        check_vma=False,
    )
```

time: 532 us -> 171 us (0.32)
  the two profiles are of different devices: /device:TPU:20 before, /device:TPU:8 now
where the time goes in v1:
time: 171 us; the launch traced here: 169 us
  matrix products  97.3 us (57%)
  other arithmetic  26.8 us (16%)
  between operations  14.3 us (8%)
  local copies, waits for them, and re-layouts  13.7 us (8%)
  loops' own time  8.54 us (5%)
  waiting for transfers between devices  4.44 us (3%)
  starting transfers between devices  4.32 us (3%)
    dot_general x29, matrix products, mul(): jnp.dot(left_mat, right_mat, precision=lax.Precision.HIGH, preferred_elem...  84.3 us
    reduce_sum x12, other arithmetic, step(): return (count + 1, total, power, jnp.sum(power * power))  25.3 us
    dot_general x6, matrix products, mul_rows(): lax.dot_general(rows, mat, (((1,), (1,)), ((), ())), precision=lax.Precis...  9.57 us
    another operation x2, loops' own time, inverse(): lax.while_loop(again, step, (0, total, power, jnp.sum(power * power)))  8.54 us
    dynamic_slice x2, local copies, waits for them, and re-layouts, block(): lax.dynamic_slice(leaf_maps, (0, leaf, row * face, col * face), (1, 1, fa...  4.88 us
    unnamed x19, local copies, waits for them, and re-layouts  4.44 us
    ppermute x3, waiting for transfers between devices, swapped(): return lax.ppermute(block, axis, route)  4.43 us
    dot_general x1, local copies, waits for them, and re-layouts, local(): jnp.einsum('mz,zbrp->mbrp', cas_rows, sources, precision=lax.Precision.HIGH)  4.38 us
  transfers between devices with their start and end apart: 4, of which 1 were waited for; matrix products, arithmetic and copies ran while one was open for 72% of the time, Pallas kernels for 0%

profile of v1, /device:TPU:8, one launch (start us, length us, event | category | flops | bytes accessed | tf_op | source)
XLA Modules:
  0.0 169.4 jit_solution(13772686677321901797)
XLA Ops:
  7.2 0.0 copy-start
  7.2 0.0 reduce-scatter.2.cloned.1.call-start
  7.2 1.5 copy-done
  8.8 3.3 %fusion.10 = f32[32,2,16,1024]{3,0,2,1:T(8,128)S(1)} fusion(f32[16,2,16,1024]{3,2,1,0:T(8,128)S(1)} %copy-done, s32[16]{0:T(128)S(1)} %iota_add_fusion, s32[32]{0:T(128)} %param.9), kind=kOutput, calls=%fused_computation.15 | convolution fusion | flops 100671488 | bytes 6291648 | tf_op jit(solution)/shard_map/mz,zbrp->mbrp/dot_general | solution.py:65
  12.1 4.4 %copy.10 = f32[32,2,16,1024]{3,2,1,0:T(8,128)} copy(f32[32,2,16,1024]{3,0,2,1:T(8,128)S(1)} %fusion.10) | data formatting | bytes 8388608 | tf_op jit(solution)/shard_map/mz,zbrp->mbrp/dot_general | solution.py:65
  16.5 0.0 reduce-scatter.2.cloned.1.call-update
  16.5 2.6 %convert_add_fusion.1 = (f32[512,512]{1,0:T(8,128)S(1)}, f32[512,512]{1,0:T(8,128)S(1)}) fusion(f32[1,2,1024,1024]{3,2,1,0:T(8,128)} %param.8, s32[]{:T(128)S(6)} %select_n.36, s32[]{:T(128)S(6)} %select_n.34, s32[]{:T(128)S(6)} %select_n.33, s32[]{:T(128)S(6)} %select_n.35), kind=kOutput, calls=%fused_computation.18 | convolution fusion | flops 806092800 | bytes 4194320 | tf_op jit(solution)/shard_map/dot_general | solution.py:18
  19.1 3.5 %fusion.15 = f32[512,512]{1,0:T(8,128)} fusion(f32[1,2,1024,1024]{3,2,1,0:T(8,128)} %param.8, s32[]{:T(128)S(6)} %select_n.36, s32[]{:T(128)S(6)} %select_n.34, s32[]{:T(128)S(6)} %select_n.35, s32[]{:T(128)S(6)} %select_n.33), kind=kOutput, calls=%fused_computation.35 | convolution fusion | flops 805306368 | bytes 3148288 | tf_op jit(solution)/shard_map/dot_general | solution.py:18
  22.6 2.5 %multiply_reduce_fusion.3 = (f32[]{:T(128)}, f32[512,512]{1,0:T(8,128)}) fusion(f32[512,512]{1,0:T(8,128)S(1)} %get-tuple-element.77), kind=kOutput, calls=%fused_computation.54 | convolution fusion | flops 805830656 | bytes 2097156 | tf_op jit(solution)/shard_map/dot_general | solution.py:18
  25.2 37.1 %while.28 = (s32[]{:T(128)}, f32[512,512]{1,0:T(8,128)S(1)}, f32[512,512]{1,0:T(8,128)}, f32[]{:T(128)}, s32[]{:T(128)}) while((s32[]{:T(128)}, f32[512,512]{1,0:T(8,128)S(1)}, f32[512,512]{1,0:T(8,128)}, f32[]{:T(128)}, s32[]{:T(128)}) %tuple.50), condition=%wide.region_3.4_spmd, body=%wide.region_1.3_spmd.sunk | while | flops 1611923456 | bytes 9437261 | solution.py:54
  25.7 3.4 %fusion.124 = f32[1024,512]{1,0:T(8,128)S(1)} fusion(f32[512,512]{1,0:T(8,128)} %get-tuple-element.151, f32[512,512]{1,0:T(8,128)S(1)} %get-tuple-element.150), kind=kOutput, calls=%fused_computation.clone.1 | convolution fusion | flops 1611137024 | bytes 4194304 | tf_op jit(solution)/shard_map/while/body/dot_general | solution.py:18
  29.1 2.1 %multiply_reduce_fusion.6 = (f32[]{:T(128)}, f32[512,512]{1,0:T(8,128)}, f32[512,512]{1,0:T(8,128)S(1)}) fusion(f32[1024,512]{1,0:T(8,128)S(1)} %fusion.124, f32[512,512]{1,0:T(8,128)S(1)} %get-tuple-element.150), kind=kLoop, calls=%fused_computation.5.clone.1 | loop fusion | flops 786431 | bytes 5242884 | tf_op jit(solution)/shard_map/while/body/reduce_sum | solution.py:52
  31.8 3.4 %fusion.124 = f32[1024,512]{1,0:T(8,128)S(1)} fusion(f32[512,512]{1,0:T(8,128)} %get-tuple-element.151, f32[512,512]{1,0:T(8,128)S(1)} %get-tuple-element.150), kind=kOutput, calls=%fused_computation.clone.1 | convolution fusion | flops 1611137024 | bytes 4194304 | tf_op jit(solution)/shard_map/while/body/dot_general | solution.py:18
  35.2 2.1 %multiply_reduce_fusion.6 = (f32[]{:T(128)}, f32[512,512]{1,0:T(8,128)}, f32[512,512]{1,0:T(8,128)S(1)}) fusion(f32[1024,512]{1,0:T(8,128)S(1)} %fusion.124, f32[512,512]{1,0:T(8,128)S(1)} %get-tuple-element.150), kind=kLoop, calls=%fused_computation.5.clone.1 | loop fusion | flops 786431 | bytes 5242884 | tf_op jit(solution)/shard_map/while/body/reduce_sum | solution.py:52
  37.9 3.4 %fusion.124 = f32[1024,512]{1,0:T(8,128)S(1)} fusion(f32[512,512]{1,0:T(8,128)} %get-tuple-element.151, f32[512,512]{1,0:T(8,128)S(1)} %get-tuple-element.150), kind=kOutput, calls=%fused_computation.clone.1 | convolution fusion | flops 1611137024 | bytes 4194304 | tf_op jit(solution)/shard_map/while/body/dot_general | solution.py:18
  41.3 2.1 %multiply_reduce_fusion.6 = (f32[]{:T(128)}, f32[512,512]{1,0:T(8,128)}, f32[512,512]{1,0:T(8,128)S(1)}) fusion(f32[1024,512]{1,0:T(8,128)S(1)} %fusion.124, f32[512,512]{1,0:T(8,128)S(1)} %get-tuple-element.150), kind=kLoop, calls=%fused_computation.5.clone.1 | loop fusion | flops 786431 | bytes 5242884 | tf_op jit(solution)/shard_map/while/body/reduce_sum | solution.py:52
  43.9 3.4 %fusion.124 = f32[1024,512]{1,0:T(8,128)S(1)} fusion(f32[512,512]{1,0:T(8,128)} %get-tuple-element.151, f32[512,512]{1,0:T(8,128)S(1)} %get-tuple-element.150), kind=kOutput, calls=%fused_computation.clone.1 | convolution fusion | flops 1611137024 | bytes 4194304 | tf_op jit(solution)/shard_map/while/body/dot_general | solution.py:18
  47.3 2.1 %multiply_reduce_fusion.6 = (f32[]{:T(128)}, f32[512,512]{1,0:T(8,128)}, f32[512,512]{1,0:T(8,128)S(1)}) fusion(f32[1024,512]{1,0:T(8,128)S(1)} %fusion.124, f32[512,512]{1,0:T(8,128)S(1)} %get-tuple-element.150), kind=kLoop, calls=%fused_computation.5.clone.1 | loop fusion | flops 786431 | bytes 5242884 | tf_op jit(solution)/shard_map/while/body/reduce_sum | solution.py:52
  50.0 3.4 %fusion.124 = f32[1024,512]{1,0:T(8,128)S(1)} fusion(f32[512,512]{1,0:T(8,128)} %get-tuple-element.151, f32[512,512]{1,0:T(8,128)S(1)} %get-tuple-element.150), kind=kOutput, calls=%fused_computation.clone.1 | convolution fusion | flops 1611137024 | bytes 4194304 | tf_op jit(solution)/shard_map/while/body/dot_general | solution.py:18
  53.4 2.1 %multiply_reduce_fusion.6 = (f32[]{:T(128)}, f32[512,512]{1,0:T(8,128)}, f32[512,512]{1,0:T(8,128)S(1)}) fusion(f32[1024,512]{1,0:T(8,128)S(1)} %fusion.124, f32[512,512]{1,0:T(8,128)S(1)} %get-tuple-element.150), kind=kLoop, calls=%fused_computation.5.clone.1 | loop fusion | flops 786431 | bytes 5242884 | tf_op jit(solution)/shard_map/while/body/reduce_sum | solution.py:52
  56.1 3.4 %fusion.124 = f32[1024,512]{1,0:T(8,128)S(1)} fusion(f32[512,512]{1,0:T(8,128)} %get-tuple-element.151, f32[512,512]{1,0:T(8,128)S(1)} %get-tuple-element.150), kind=kOutput, calls=%fused_computation.clone.1 | convolution fusion | flops 1611137024 | bytes 4194304 | tf_op jit(solution)/shard_map/while/body/dot_general | solution.py:18
  59.5 2.1 %multiply_reduce_fusion.6 = (f32[]{:T(128)}, f32[512,512]{1,0:T(8,128)}, f32[512,512]{1,0:T(8,128)S(1)}) fusion(f32[1024,512]{1,0:T(8,128)S(1)} %fusion.124, f32[512,512]{1,0:T(8,128)S(1)} %get-tuple-element.150), kind=kLoop, calls=%fused_computation.5.clone.1 | loop fusion | flops 786431 | bytes 5242884 | tf_op jit(solution)/shard_map/while/body/reduce_sum | solution.py:52
  62.3 2.2 %fusion.13 = f32[512,512]{1,0:T(8,128)S(1)} fusion(f32[512,512]{1,0:T(8,128)S(1)} %get-tuple-element.46, f32[1,2,1024,1024]{3,2,1,0:T(8,128)} %param.8, s32[]{:T(128)S(6)} %select_n.36, s32[]{:T(128)S(6)} %select_n.35, s32[]{:T(128)S(6)} %select_n.34), kind=kOutput, calls=%fused_computation.33 | convolution fusion | flops 805306368 | bytes 3145740 | tf_op jit(solution)/shard_map/dot_general | solution.py:18
  64.6 3.9 %convolution_add_fusion.1 = f32[512,512]{1,0:T(8,128)} fusion(f32[512,512]{1,0:T(8,128)S(1)} %fusion.13, f32[512,512]{1,0:T(8,128)} %fusion.15, f32[1,2,1024,1024]{3,2,1,0:T(8,128)} %param.8, s32[]{:T(128)S(6)} %select_n.36, s32[]{:T(128)S(6)} %select_n.35), kind=kOutput, calls=%fused_computation.22 | convolution fusion | flops 805568512 | bytes 4194312 | tf_op jit(solution)/shard_map/dot_general | solution.py:18
  68.5 2.2 %collective-permute-start = (f32[512,512]{1,0:T(8,128)}, f32[512,512]{1,0:T(8,128)}, u32[]{:S(2)}, u32[]{:S(2)}) collective-permute-start(f32[512,512]{1,0:T(8,128)} %convolution_add_fusion.1), channel_id=1, source_target_pairs={{0,1},{1,0},{2,3},{3,2},{4,5},{5,4},{6,7},{7,6},{8,9},{9,8},{10,11... | collective-permute-start | bytes 3145736 | tf_op jit(solution)/shard_map/ppermute | solution.py:14
  70.7 3.2 %convolution_negate_fusion.1 = f32[512,512]{1,0:T(8,128)} fusion(f32[512,512]{1,0:T(8,128)S(1)} %fusion.13, f32[1,2,1024,1024]{3,2,1,0:T(8,128)} %param.8, s32[]{:T(128)S(6)} %select_n.33, s32[]{:T(128)S(6)} %select_n.35, s32[]{:T(128)S(6)} %select_n.34), kind=kOutput, calls=%fused_computation.21 | convolution fusion | flops 805568512 | bytes 3145740 | tf_op jit(solution)/shard_map/dot_general | solution.py:18
  73.9 2.3 %constant_dynamic-slice_fusion = f32[1,1,512,512]{3,2,1,0:T(8,128)} fusion(f32[1,2,1024,1024]{3,2,1,0:T(8,128)} %param.8, s32[]{:T(128)S(6)} %select_n.33, s32[]{:T(128)S(6)} %select_n.34), kind=kLoop, calls=%fused_computation.105 | loop fusion | bytes 2097160 | tf_op jit(solution)/shard_map/dynamic_slice | solution.py:74
  76.2 2.6 %copy.8 = f32[1,1,512,512]{2,3,1,0:T(8,128)} copy(f32[1,1,512,512]{3,2,1,0:T(8,128)} %constant_dynamic-slice_fusion) | data formatting | bytes 2097152 | tf_op jit(solution)/shard_map/dynamic_slice | solution.py:74
  78.8 2.6 %fusion.25 = f32[512,512]{1,0:T(8,128)S(1)} fusion(f32[1,2,1024,1024]{3,2,1,0:T(8,128)} %param.8, s32[]{:T(128)S(6)} %select_n.36, s32[]{:T(128)S(6)} %select_n.34, s32[]{:T(128)S(6)} %select_n.33, s32[]{:T(128)S(6)} %select_n.35), kind=kOutput, calls=%fused_computation.45 | convolution fusion | flops 805306368 | bytes 3148288 | tf_op jit(solution)/shard_map/dot_general | solution.py:18
  81.4 2.6 %convolution_negate_fusion.2 = f32[512,512]{1,0:T(8,128)S(1)} fusion(f32[1,2,1024,1024]{3,2,1,0:T(8,128)} %param.8, s32[]{:T(128)S(6)} %select_n.36, s32[]{:T(128)S(6)} %select_n.34, s32[]{:T(128)S(6)} %select_n.35, s32[]{:T(128)S(6)} %select_n.33), kind=kOutput, calls=%fused_computation.24 | convolution fusion | flops 805568512 | bytes 3148800 | tf_op jit(solution)/shard_map/dot_general | solution.py:18
  84.0 1.0 fusion.80
  85.0 3.6 %convolution_add_fusion.2 = f32[512,512]{0,1:T(8,128)} fusion(f32[512,512]{1,0:T(8,128)S(1)} %fusion.80, f32[1,1,512,512]{2,3,1,0:T(8,128)S(1)} %copy-done.7, f32[1,2,1024,1024]{3,2,1,0:T(8,128)} %param.8, s32[]{:T(128)S(6)} %select_n.33, s32[]{:T(128)S(6)} %select_n.35, s32[]{:T(128)S(6)} %select_n.34), kind=kOutput, calls=%fused_computation.25 | convolution fusion | flops 805568512 | bytes 4194316 | tf_op jit(solution)/shard_map/dot_general | solution.py:18
  88.7 2.0 %convolution_subtract_fusion = f32[512,512]{1,0:T(8,128)} fusion(f32[512,512]{1,0:T(8,128)S(1)} %convolution_negate_fusion.2, f32[512,512]{1,0:T(8,128)S(1)} %fusion.80, f32[512,512]{1,0:T(8,128)S(1)} %copy-done.6), kind=kOutput, calls=%fused_computation.23 | convolution fusion | flops 805568512 | bytes 4194304 | tf_op jit(solution)/shard_map/dot_general | solution.py:18
  90.6 4.4 %collective-permute-done = f32[512,512]{1,0:T(8,128)} collective-permute-done((f32[512,512]{1,0:T(8,128)}, f32[512,512]{1,0:T(8,128)}, u32[]{:S(2)}, u32[]{:S(2)}) %collective-permute-start) | collective-permute-done | bytes 1048608 | tf_op jit(solution)/shard_map/ppermute | solution.py:14
  95.1 2.5 %convert_add_fusion = (f32[512,512]{1,0:T(8,128)S(1)}, f32[512,512]{1,0:T(8,128)S(1)}) fusion(f32[512,512]{1,0:T(8,128)} %collective-permute-done, f32[512,512]{1,0:T(8,128)} %convolution_add_fusion.1), kind=kOutput, calls=%fused_computation.17 | convolution fusion | flops 806092800 | bytes 4194304 | tf_op jit(solution)/shard_map/dot_general | solution.py:18
  97.6 2.6 %multiply_reduce_fusion.2 = (f32[]{:T(128)}, f32[512,512]{1,0:T(8,128)}) fusion(f32[512,512]{1,0:T(8,128)S(1)} %get-tuple-element.81), kind=kOutput, calls=%fused_computation.52 | convolution fusion | flops 805830656 | bytes 2097156 | tf_op jit(solution)/shard_map/dot_general | solution.py:18
  100.2 37.5 %while.29 = (s32[]{:T(128)}, f32[512,512]{1,0:T(8,128)S(1)}, f32[512,512]{1,0:T(8,128)}, f32[]{:T(128)}, s32[]{:T(128)}) while((s32[]{:T(128)}, f32[512,512]{1,0:T(8,128)S(1)}, f32[512,512]{1,0:T(8,128)}, f32[]{:T(128)}, s32[]{:T(128)}) %tuple.53), condition=%wide.region_7.8_spmd, body=%wide.region_5.7_spmd.sunk | while | flops 1611923456 | bytes 9437261 | solution.py:54
  101.0 3.4 %fusion.127 = f32[1024,512]{1,0:T(8,128)S(1)} fusion(f32[512,512]{1,0:T(8,128)} %get-tuple-element.166, f32[512,512]{1,0:T(8,128)S(1)} %get-tuple-element.165), kind=kOutput, calls=%fused_computation.7.clone.1 | convolution fusion | flops 1611137024 | bytes 4194304 | tf_op jit(solution)/shard_map/while/body/dot_general | solution.py:18
  104.4 2.1 %multiply_reduce_fusion.7 = (f32[]{:T(128)}, f32[512,512]{1,0:T(8,128)}, f32[512,512]{1,0:T(8,128)S(1)}) fusion(f32[1024,512]{1,0:T(8,128)S(1)} %fusion.127, f32[512,512]{1,0:T(8,128)S(1)} %get-tuple-element.165), kind=kLoop, calls=%fused_computation.12.clone.1 | loop fusion | flops 786431 | bytes 5242884 | tf_op jit(solution)/shard_map/while/body/reduce_sum | solution.py:52
  107.1 3.4 %fusion.127 = f32[1024,512]{1,0:T(8,128)S(1)} fusion(f32[512,512]{1,0:T(8,128)} %get-tuple-element.166, f32[512,512]{1,0:T(8,128)S(1)} %get-tuple-element.165), kind=kOutput, calls=%fused_computation.7.clone.1 | convolution fusion | flops 1611137024 | bytes 4194304 | tf_op jit(solution)/shard_map/while/body/dot_general | solution.py:18
  110.5 2.1 %multiply_reduce_fusion.7 = (f32[]{:T(128)}, f32[512,512]{1,0:T(8,128)}, f32[512,512]{1,0:T(8,128)S(1)}) fusion(f32[1024,512]{1,0:T(8,128)S(1)} %fusion.127, f32[512,512]{1,0:T(8,128)S(1)} %get-tuple-element.165), kind=kLoop, calls=%fused_computation.12.clone.1 | loop fusion | flops 786431 | bytes 5242884 | tf_op jit(solution)/shard_map/while/body/reduce_sum | solution.py:52
  113.3 3.4 %fusion.127 = f32[1024,512]{1,0:T(8,128)S(1)} fusion(f32[512,512]{1,0:T(8,128)} %get-tuple-element.166, f32[512,512]{1,0:T(8,128)S(1)} %get-tuple-element.165), kind=kOutput, calls=%fused_computation.7.clone.1 | convolution fusion | flops 1611137024 | bytes 4194304 | tf_op jit(solution)/shard_map/while/body/dot_general | solution.py:18
  116.7 2.1 %multiply_reduce_fusion.7 = (f32[]{:T(128)}, f32[512,512]{1,0:T(8,128)}, f32[512,512]{1,0:T(8,128)S(1)}) fusion(f32[1024,512]{1,0:T(8,128)S(1)} %fusion.127, f32[512,512]{1,0:T(8,128)S(1)} %get-tuple-element.165), kind=kLoop, calls=%fused_computation.12.clone.1 | loop fusion | flops 786431 | bytes 5242884 | tf_op jit(solution)/shard_map/while/body/reduce_sum | solution.py:52
  119.4 3.4 %fusion.127 = f32[1024,512]{1,0:T(8,128)S(1)} fusion(f32[512,512]{1,0:T(8,128)} %get-tuple-element.166, f32[512,512]{1,0:T(8,128)S(1)} %get-tuple-element.165), kind=kOutput, calls=%fused_computation.7.clone.1 | convolution fusion | flops 1611137024 | bytes 4194304 | tf_op jit(solution)/shard_map/while/body/dot_general | solution.py:18
  122.8 2.1 %multiply_reduce_fusion.7 = (f32[]{:T(128)}, f32[512,512]{1,0:T(8,128)}, f32[512,512]{1,0:T(8,128)S(1)}) fusion(f32[1024,512]{1,0:T(8,128)S(1)} %fusion.127, f32[512,512]{1,0:T(8,128)S(1)} %get-tuple-element.165), kind=kLoop, calls=%fused_computation.12.clone.1 | loop fusion | flops 786431 | bytes 5242884 | tf_op jit(solution)/shard_map/while/body/reduce_sum | solution.py:52
  125.5 3.4 %fusion.127 = f32[1024,512]{1,0:T(8,128)S(1)} fusion(f32[512,512]{1,0:T(8,128)} %get-tuple-element.166, f32[512,512]{1,0:T(8,128)S(1)} %get-tuple-element.165), kind=kOutput, calls=%fused_computation.7.clone.1 | convolution fusion | flops 1611137024 | bytes 4194304 | tf_op jit(solution)/shard_map/while/body/dot_general | solution.py:18
  128.9 2.1 %multiply_reduce_fusion.7 = (f32[]{:T(128)}, f32[512,512]{1,0:T(8,128)}, f32[512,512]{1,0:T(8,128)S(1)}) fusion(f32[1024,512]{1,0:T(8,128)S(1)} %fusion.127, f32[512,512]{1,0:T(8,128)S(1)} %get-tuple-element.165), kind=kLoop, calls=%fused_computation.12.clone.1 | loop fusion | flops 786431 | bytes 5242884 | tf_op jit(solution)/shard_map/while/body/reduce_sum | solution.py:52
  131.6 3.4 %fusion.127 = f32[1024,512]{1,0:T(8,128)S(1)} fusion(f32[512,512]{1,0:T(8,128)} %get-tuple-element.166, f32[512,512]{1,0:T(8,128)S(1)} %get-tuple-element.165), kind=kOutput, calls=%fused_computation.7.clone.1 | convolution fusion | flops 1611137024 | bytes 4194304 | tf_op jit(solution)/shard_map/while/body/dot_general | solution.py:18
  135.0 2.1 %multiply_reduce_fusion.7 = (f32[]{:T(128)}, f32[512,512]{1,0:T(8,128)}, f32[512,512]{1,0:T(8,128)S(1)}) fusion(f32[1024,512]{1,0:T(8,128)S(1)} %fusion.127, f32[512,512]{1,0:T(8,128)S(1)} %get-tuple-element.165), kind=kLoop, calls=%fused_computation.12.clone.1 | loop fusion | flops 786431 | bytes 5242884 | tf_op jit(solution)/shard_map/while/body/reduce_sum | solution.py:52
  137.7 0.0 copy-start.8
  137.7 2.3 %fusion.81 = f32[512,512]{1,0:T(8,128)S(1)} fusion(f32[512,512]{1,0:T(8,128)} %convolution_subtract_fusion, f32[512,512]{1,0:T(8,128)S(1)} %get-tuple-element.47), kind=kOutput, calls=%fused_computation.112 | convolution fusion | flops 805306368 | bytes 3145728 | tf_op jit(solution)/shard_map/dot_general | solution.py:18
  140.1 2.9 %fusion.82 = f32[512,512]{1,0:T(8,128)S(1)} fusion(f32[512,512]{1,0:T(8,128)} %collective-permute-done, f32[512,512]{1,0:T(8,128)} %convolution_negate_fusion.1), kind=kOutput, calls=%fused_computation.113 | convolution fusion | flops 805306368 | bytes 3145728 | tf_op jit(solution)/shard_map/dot_general | solution.py:18
  143.0 1.1 convolution_add_fusion
  144.1 0.0 collective-permute-done.1
  144.1 2.3 %select_bitcast_fusion.1 = (f32[1,1,512,512]{2,3,1,0:T(8,128)S(1)}, f32[1,1,512,512]{2,3,1,0:T(8,128)S(1)}) fusion(f32[512,512]{0,1:T(8,128)S(1)} %convolution_add_fusion, pred[]{:T(512)S(6)} %eq.13, f32[512,512]{1,0:T(8,128)S(1)} %fusion.81, f32[512,512]{1,0:T(8,128)} %collective-permute-done.1), kind=kOutput, calls=%fused_computation.51 | convolution fusion | flops 806092800 | bytes 5242881 | tf_op jit(solution)/shard_map/dot_general | solution.py:18
  146.4 1.5 maximum_multiply_fusion
  148.0 2.9 %copy.11 = f32[1,1,512,1024]{3,2,1,0:T(8,128)} copy(f32[1,1,512,1024]{2,3,1,0:T(8,128)} %maximum_multiply_fusion) | data formatting | bytes 4194304
  150.9 1.8 %convolution_subtract_fusion.4 = f32[16,512]{1,0:T(8,128)S(1)} fusion(f32[1,2,1024,1024]{3,2,1,0:T(8,128)} %param.8, s32[]{:T(128)S(6)} %select_n.33, s32[]{:T(128)S(6)} %select_n.35, f32[1,2,16,1024]{3,2,1,0:T(8,128)} %reduce-scatter.2.cloned.1.call-done, s32[]{:T(128)S(6)} %select_n.36, s32[]{:T(128)S(6)} %select_n.34), kind=kOutput, calls=%fused_computation.32 | convolution fusion | flops 25174016 | bytes 1149952 | tf_op jit(solution)/shard_map/dot_general | solution.py:24
  152.7 1.3 convolution_subtract_fusion.2
  154.0 2.1 %collective-permute-start.2 = (f32[16,512]{1,0:T(8,128)S(1)}, f32[16,512]{1,0:T(8,128)S(1)}, u32[]{:S(2)}, u32[]{:S(2)}) collective-permute-start(f32[16,512]{1,0:T(8,128)S(1)} %convolution_subtract_fusion.2), channel_id=1, source_target_pairs={{0,1},{1,0},{2,3},{3,2},{4,5},{5,4},{6,7},{7,6},{8,9},{9,8},{10,11... | collective-permute-start | bytes 98312 | tf_op jit(solution)/shard_map/ppermute | solution.py:14
  156.1 1.8 %convolution_add_fusion.4 = f32[16,512]{1,0:T(8,128)S(1)} fusion(f32[16,512]{1,0:T(8,128)S(1)} %convolution_subtract_fusion.4, f32[512,512]{1,0:T(8,128)} %copy-done.3, f32[1,2,16,1024]{3,2,1,0:T(8,128)} %reduce-scatter.2.cloned.1.call-done, s32[]{:T(128)S(6)} %select_n.33, s32[]{:T(128)S(6)} %select_n.34), kind=kOutput, calls=%fused_computation.31 | convolution fusion | flops 25174016 | bytes 1146888 | tf_op jit(solution)/shard_map/dot_general | solution.py:24
  157.8 1.8 %convolution_subtract_fusion.3 = f32[16,512]{1,0:T(8,128)S(1)} fusion(f32[16,512]{1,0:T(8,128)S(1)} %convolution_add_fusion.4, f32[1,2,1024,1024]{3,2,1,0:T(8,128)} %param.8, s32[]{:T(128)S(6)} %select_n.33, s32[]{:T(128)S(6)} %select_n.34, s32[]{:T(128)S(6)} %select_n.35, f32[1,2,16,1024]{3,2,1,0:T(8,128)} %reduce-scatter.2.cloned.1.call-done, ...), kind=kOutput, calls=%fused_computation.30 | convolution fusion | flops 25174016 | bytes 1149440 | tf_op jit(solution)/shard_map/dot_general | solution.py:24
  159.7 1.8 %convolution_subtract_fusion.1 = f32[16,512]{1,0:T(8,128)S(1)} fusion(f32[16,512]{1,0:T(8,128)S(1)} %collective-permute-done.2, f32[16,512]{1,0:T(8,128)S(1)} %convolution_subtract_fusion.2, f32[512,512]{1,0:T(8,128)} %collective-permute-done), kind=kOutput, calls=%fused_computation.28 | convolution fusion | flops 25174016 | bytes 1146880 | tf_op jit(solution)/shard_map/dot_general | solution.py:24
  161.4 1.2 fusion.12
  (19 shorter events, 0.0 us)
Async XLA Ops:
  7.2 1.6 copy-start
  7.2 143.7 %reduce-scatter.2.cloned.1.call-start = ((), (), s32[]{:S(2)}) async-start(), calls=%async_computation.1 | async-start | bytes 4325376 | tf_op jit(solution)/shard_map/reduce_scatter | solution.py:64
  64.6 6.1 %copy-start.1 = (f32[512,512]{1,0:T(8,128)}, f32[512,512]{1,0:T(8,128)S(1)}, u32[]{:S(2)}) copy-start(f32[512,512]{1,0:T(8,128)S(1)} %fusion.13) | copy-start | bytes 3145732
  68.5 26.6 %collective-permute-start = (f32[512,512]{1,0:T(8,128)}, f32[512,512]{1,0:T(8,128)}, u32[]{:S(2)}, u32[]{:S(2)}) collective-permute-start(f32[512,512]{1,0:T(8,128)} %convolution_add_fusion.1), channel_id=1, source_target_pairs={{0,1},{1,0},{2,3},{3,2},{4,5},{5,4},{6,7},{7,6},{8,9},{9,8},{10,11... | collective-permute-start | bytes 3145736 | tf_op jit(solution)/shard_map/ppermute | solution.py:14
  73.9 70.2 %collective-permute-start.1 = (f32[512,512]{1,0:T(8,128)}, f32[512,512]{1,0:T(8,128)}, u32[]{:S(2)}, u32[]{:S(2)}) collective-permute-start(f32[512,512]{1,0:T(8,128)} %convolution_negate_fusion.1), channel_id=1, source_target_pairs={{0,1},{1,0},{2,3},{3,2},{4,5},{5,4},{6,7},{7,6},{8,9},{9,8},{10,11... | collective-permute-start | bytes 3145736 | tf_op jit(solution)/shard_map/ppermute | solution.py:14
  78.8 6.2 %copy-start.7 = (f32[1,1,512,512]{2,3,1,0:T(8,128)S(1)}, f32[1,1,512,512]{2,3,1,0:T(8,128)}, u32[]{:S(2)}) copy-start(f32[1,1,512,512]{2,3,1,0:T(8,128)} %copy.8) | copy-start | bytes 3145732
  84.0 4.7 %copy-start.6 = (f32[512,512]{1,0:T(8,128)S(1)}, f32[512,512]{1,0:T(8,128)}, u32[]{:S(2)}) copy-start(f32[512,512]{1,0:T(8,128)} %fusion.15) | copy-start | bytes 3145732
  85.0 5.6 %copy-start.3 = (f32[512,512]{1,0:T(8,128)}, f32[512,512]{1,0:T(8,128)S(1)}, u32[]{:S(2)}) copy-start(f32[512,512]{1,0:T(8,128)S(1)} %fusion.80) | copy-start | bytes 3145732
  137.7 5.3 %copy-start.8 = (f32[512,512]{0,1:T(8,128)S(1)}, f32[512,512]{0,1:T(8,128)}, u32[]{:S(2)}) copy-start(f32[512,512]{0,1:T(8,128)} %convolution_add_fusion.2) | copy-start | bytes 3145732
  140.1 6.3 %copy-start.4 = (f32[512,512]{1,0:T(8,128)}, f32[512,512]{1,0:T(8,128)S(1)}, u32[]{:S(2)}) copy-start(f32[512,512]{1,0:T(8,128)S(1)} %fusion.81) | copy-start | bytes 3145732
  146.4 6.3 %copy-start.2 = (f32[512,512]{1,0:T(8,128)S(1)}, f32[512,512]{1,0:T(8,128)}, u32[]{:S(2)}) copy-start(f32[512,512]{1,0:T(8,128)} %copy-done.1) | copy-start | bytes 3145732
  150.9 10.5 %copy-start.5 = (f32[512,512]{1,0:T(8,128)S(1)}, f32[512,512]{1,0:T(8,128)}, u32[]{:S(2)}) copy-start(f32[512,512]{1,0:T(8,128)} %copy-done.4) | copy-start | bytes 3145732
  154.0 5.6 %collective-permute-start.2 = (f32[16,512]{1,0:T(8,128)S(1)}, f32[16,512]{1,0:T(8,128)S(1)}, u32[]{:S(2)}, u32[]{:S(2)}) collective-permute-start(f32[16,512]{1,0:T(8,128)S(1)} %convolution_subtract_fusion.2), channel_id=1, source_target_pairs={{0,1},{1,0},{2,3},{3,2},{4,5},{5,4},{6,7},{7,6},{8,9},{9,8},{10,11... | collective-permute-start | bytes 98312 | tf_op jit(solution)/shard_map/ppermute | solution.py:14
Sparse Core Ops, SparseCore 0:
  16.6 125.2 reduce-scatter.1

commit v2 on v1

v2 whole, which is shorter than its diff:
```python
import jax
import jax.numpy as jnp
from jax import lax
from jax.experimental import pallas as pl
from jax.experimental.pallas import tpu as pltpu
from jax.sharding import PartitionSpec as P

NZ = 512
MESH = pl.DeviceIdType.MESH
F32 = jnp.float32
BF16 = jnp.bfloat16
HALF = 256
ROUGH = 4e-4
FINE = 1e-10
VMEM_LIMIT = 44 * 1024 * 1024


def swapped(block, axis):
    count = lax.axis_size(axis)
    route = []
    for low in range(0, count, 2):
        route += [(low, low + 1), (low + 1, low)]
    return lax.ppermute(block, axis, route)


def cas_table(mode_list, z_index, length_z):
    phase = mode_list[:, None] * z_index[None, :] % length_z
    angle = phase.astype(F32) * (2.0 * jnp.pi / length_z)
    return (jnp.cos(angle) + jnp.sin(angle)) / jnp.sqrt(jnp.float32(length_z))


def split(value):
    high = value.astype(BF16)
    return high, (value - high.astype(F32)).astype(BF16)


def put_left(ref, start, value):
    face = value.shape[1]
    high, low = split(value)
    rows = pl.ds(start, value.shape[0])
    ref[rows, 0:face] = high
    ref[rows, face : 2 * face] = high
    ref[rows, 2 * face : 3 * face] = low


def put_right(ref, start, value):
    face = ref.shape[0] // 3
    high, low = split(value)
    count = value.shape[0]
    ref[pl.ds(start, count), :] = high
    ref[pl.ds(face + start, count), :] = low
    ref[pl.ds(2 * face + start, count), :] = high


def fill(put, ref, source):
    for start in range(0, source.shape[0], HALF):
        put(ref, start, source[start : start + HALF, :])


def product(left, right, start):
    return jnp.dot(left[start : start + HALF, :], right[...], preferred_element_type=F32)


def halves(face):
    return range(0, face, HALF)


def eye_rows(start, face):
    row = lax.broadcasted_iota(jnp.int32, (HALF, face), 0) + start
    col = lax.broadcasted_iota(jnp.int32, (HALF, face), 1)
    return jnp.where(row == col, 1.0, 0.0).astype(F32)


def invert(k_left, total, power, rough, left, right, spare):
    face = total.shape[0]

    def square():
        return [
            jnp.dot(power[s : s + HALF, :], power[...], preferred_element_type=F32)
            for s in halves(face)
        ]

    def keep(parts):
        size = 0.0
        for s, part in zip(halves(face), parts):
            power[s : s + HALF, :] = part.astype(BF16)
            size += jnp.sum(part * part)
        return size

    size = keep(square())

    def rough_step(state):
        count, _ = state
        for s in halves(face):
            rough[s : s + HALF, :] = total[s : s + HALF, :].astype(BF16)
        for s in halves(face):
            total[s : s + HALF, :] += jnp.dot(
                rough[s : s + HALF, :], power[...], preferred_element_type=F32
            )
        return count + 1, keep(square())

    lax.while_loop(
        lambda state: (state[1] > ROUGH) & (state[0] < 12), rough_step, (jnp.int32(0), size)
    )

    def residual():
        size = 0.0
        fill(put_right, right, total)
        for s in halves(face):
            part = (
                product(k_left, right, s) - total[s : s + HALF, :] + eye_rows(s, face)
            )
            spare[s : s + HALF, :] = part
            size += jnp.sum(part * part)
        return size

    first = residual()
    bad = jnp.logical_not(first < 0.25)

    def careful():
        for s in halves(face):
            kept = k_left[s : s + HALF, 0:face].astype(F32)
            kept += k_left[s : s + HALF, 2 * face : 3 * face].astype(F32)
            spare[s : s + HALF, :] = kept
            total[s : s + HALF, :] = kept + eye_rows(s, face)

        def raise_power():
            fill(put_left, left, spare)
            fill(put_right, right, spare)
            size = 0.0
            for s in halves(face):
                part = product(left, right, s)
                spare[s : s + HALF, :] = part
                size += jnp.sum(part * part)
            return size

        def step(state):
            count, _ = state
            fill(put_left, left, total)
            fill(put_right, right, spare)
            for s in halves(face):
                total[s : s + HALF, :] += product(left, right, s)
            return count + 1, raise_power()

        lax.while_loop(
            lambda state: (state[1] > 1e-15) & (state[0] < 48),
            step,
            (jnp.int32(0), raise_power()),
        )
        return residual()

    first = lax.cond(bad, careful, lambda: first)

    def newton(state):
        count, size, _ = state
        for s in halves(face):
            rough[s : s + HALF, :] = spare[s : s + HALF, :].astype(BF16)
        second = 0.0
        for s in halves(face):
            part = jnp.dot(rough[s : s + HALF, :], rough[...], preferred_element_type=F32)
            second += jnp.sum(part * part)
            put_right(right, s, spare[s : s + HALF, :] + part)
        fill(put_left, left, total)
        for s in halves(face):
            total[s : s + HALF, :] += product(left, right, s)
        bound = size * second
        size = lax.cond(bound > FINE, residual, lambda: size)
        return count + 1, size, bound

    lax.while_loop(
        lambda state: (state[2] > FINE) & (state[0] < 12),
        newton,
        (jnp.int32(0), first, jnp.float32(1.0)),
    )


def near_kernel(maps, o_33, o_31, gain, inv, through, *scratch):
    a_33, b_33, b_32, b_23, b_22, a_31 = scratch[:6]
    l_one, l_two, k_left, r_one, r_two, power, rough, spare, sems = scratch[6:]
    face = o_33.shape[0]
    far = lax.axis_index("box") % 2
    near = 1 - far

    def fetch(slot, leaf, row, col, dst):
        view = maps.at[
            0,
            leaf,
            pl.ds(pl.multiple_of(row * face, face), face),
            pl.ds(pl.multiple_of(col * face, face), face),
        ]
        copy = pltpu.make_async_copy(view, dst, sems.at[slot])
        copy.start()
        return copy

    copies = [
        fetch(0, far, near, near, a_33),
        fetch(1, near, far, far, b_33),
        fetch(2, near, far, near, b_32),
        fetch(3, near, near, far, b_23),
        fetch(4, near, near, near, b_22),
        fetch(5, far, near, far, a_31),
    ]
    copies[0].wait()
    fill(put_left, l_one, a_33)
    copies[1].wait()
    fill(put_right, r_one, b_33)
    for s in halves(face):
        part = product(l_one, r_one, s)
        put_left(k_left, s, part)
        power[s : s + HALF, :] = part.astype(BF16)
        inv[s : s + HALF, :] = part + eye_rows(s, face)
    copies[2].wait()
    fill(put_right, r_one, b_32)
    for s in halves(face):
        part = product(l_one, r_one, s)
        through[s : s + HALF, :] = part
    fill(put_right, r_two, through)
    invert(k_left, inv, power, rough, l_one, r_one, spare)
    copies[3].wait()
    fill(put_left, l_one, b_23)
    fill(put_right, r_one, inv)
    for s in halves(face):
        part = product(l_one, r_one, s)
        gain[s : s + HALF, :] = part
        put_left(l_two, s, part)
    copies[4].wait()
    for s in halves(face):
        o_33[s : s + HALF, :] = b_22[s : s + HALF, :] + product(l_two, r_two, s)
    copies[5].wait()
    fill(put_right, r_one, a_31)
    for s in halves(face):
        o_31[s : s + HALF, :] = -product(l_two, r_one, s)


def far_kernel(maps, inv, through, o_11, o_13, gain, *scratch):
    a_13, b_33, b_32, a_11, a_31, left, r_one, r_two, sems = scratch
    face = o_11.shape[0]
    far = lax.axis_index("box") % 2
    near = 1 - far

    def fetch(slot, leaf, row, col, dst):
        view = maps.at[
            0,
            leaf,
            pl.ds(pl.multiple_of(row * face, face), face),
            pl.ds(pl.multiple_of(col * face, face), face),
        ]
        copy = pltpu.make_async_copy(view, dst, sems.at[slot])
        copy.start()
        return copy

    copies = [
        fetch(0, far, far, near, a_13),
        fetch(1, near, far, far, b_33),
        fetch(2, near, far, near, b_32),
        fetch(3, far, far, far, a_11),
        fetch(4, far, near, far, a_31),
    ]
    copies[0].wait()
    fill(put_left, left, a_13)
    copies[1].wait()
    fill(put_right, r_one, b_33)
    copies[2].wait()
    fill(put_right, r_two, b_32)
    for s in halves(face):
        gain[s : s + HALF, :] = product(left, r_one, s)
        o_13[s : s + HALF, :] = -product(left, r_two, s)
    fill(put_left, left, gain)
    fill(put_right, r_one, inv)
    for s in halves(face):
        gain[s : s + HALF, :] = product(left, r_one, s)
    fill(put_left, left, gain)
    copies[4].wait()
    fill(put_right, r_one, a_31)
    fill(put_right, r_two, through)
    copies[3].wait()
    for s in halves(face):
        o_11[s : s + HALF, :] = a_11[s : s + HALF, :] + product(left, r_one, s)
        o_13[s : s + HALF, :] -= product(left, r_two, s)


def rows_times(rows, mat):
    r_high, r_low = split(rows)
    m_high, m_low = split(mat)

    def dot(left, right):
        return lax.dot_general(
            left, right, (((1,), (1,)), ((), ())), preferred_element_type=F32
        )

    return dot(r_high, m_high) + (dot(r_low, m_high) + dot(r_high, m_low))


def data_kernel(maps, spectral, near_gain, far_gain, near_data, far_data, a_33, a_13, sems):
    face = near_gain.shape[0]
    far = lax.axis_index("box") % 2
    near = 1 - far

    def fetch(slot, leaf, row, col, dst):
        view = maps.at[
            0,
            leaf,
            pl.ds(pl.multiple_of(row * face, face), face),
            pl.ds(pl.multiple_of(col * face, face), face),
        ]
        copy = pltpu.make_async_copy(view, dst, sems.at[slot])
        copy.start()
        return copy

    copies = [fetch(0, far, near, near, a_33), fetch(1, far, far, near, a_13)]

    def info(leaf, side):
        return spectral[leaf, :, pl.ds(pl.multiple_of(side * face, face), face)]

    h_1, h_3 = info(far, far), info(far, near)
    g_3, g_2 = info(near, far), info(near, near)
    copies[0].wait()
    jump = h_3 - rows_times(g_3, a_33[...])
    near_data[...] = g_2 - rows_times(jump, near_gain[...])
    copies[1].wait()
    far_data[...] = h_1 + rows_times(jump, far_gain[...]) - rows_times(g_3, a_13[...])


def top_kernel(y_33, o_33, o_31, o_13, o_11, out, gain, *scratch):
    own, inv, l_one, k_left, r_one, r_two, power, rough, spare, sem = scratch
    face = y_33.shape[0]
    far = lax.axis_index("box") % 2
    fill(put_left, l_one, y_33)
    fill(put_right, r_one, o_33)
    for s in halves(face):
        part = product(l_one, r_one, s)
        put_left(k_left, s, part)
        power[s : s + HALF, :] = part.astype(BF16)
        inv[s : s + HALF, :] = part + eye_rows(s, face)
    fill(put_right, r_one, o_31)
    for s in halves(face):
        put_right(r_two, s, product(l_one, r_one, s))
    invert(k_left, inv, power, rough, l_one, r_one, spare)
    fill(put_left, l_one, o_13)
    fill(put_right, r_one, inv)
    for s in halves(face):
        part = product(l_one, r_one, s)
        gain[s : s + HALF, :] = part
        put_left(k_left, s, part)
    scale = (2.0 * face) ** 0.5
    for s in halves(face):
        own[s : s + HALF, :] = (o_11[s : s + HALF, :] + product(k_left, r_two, s)) * scale
    copy = pltpu.make_async_copy(
        own, out.at[:, pl.ds(pl.multiple_of(far * face, face), face)], sem
    )
    copy.start()
    copy.wait()


def last_kernel(
    y_32, gain, y_33, near_data, far_data, other_data, _, out, data, other, left, right, sem
):
    face = gain.shape[0]
    near = 1 - lax.axis_index("box") % 2
    scale = (2.0 * face) ** 0.5
    fill(put_left, left, gain)
    fill(put_right, right, y_32)
    for s in halves(face):
        other[s : s + HALF, :] = product(left, right, s) * -scale
    copy = pltpu.make_async_copy(
        other, out.at[:, pl.ds(pl.multiple_of(near * face, face), face)], sem
    )
    copy.start()
    jump = rows_times(near_data[...], y_33[...]) - other_data[...]
    data[...] = far_data[...] + rows_times(jump, gain[...])
    copy.wait()


def sums_kernel(cas, own, other, out, sent, got, mine, side_sent, side_got, send_sem, recv_sem):
    planes = own.shape[0]
    here = lax.axis_index("gz")
    core, z, x = here % 2, here // 2 % 8, here // 16

    def device(x_at, z_at):
        return {"gz": x_at * 16 + z_at * 2 + core}

    ring = (device(x, (z + 1) % 8), device(x, (z + 7) % 8))
    beside = device(1 - x, z)
    barrier = pltpu.get_barrier_semaphore()
    for target in (*ring, beside):
        pl.semaphore_signal(barrier, inc=1, device_id=target, device_id_type=MESH)

    def term(x_to, z_to, store):
        row = (x_to * 8 + z_to) * (2 * planes)

        def block(part, carry):
            rows = pl.ds(pl.multiple_of(part * 8, 8), 8)
            total = cas[row] * own[0, rows, :]
            for k in range(1, planes):
                total += cas[row + k] * own[k, rows, :]
            for k in range(planes):
                total += cas[row + planes + k] * other[k, rows, :]
            store(rows, total)
            return carry

        lax.fori_loop(0, own.shape[1] // 8, block, 0)

    def message(way, index):
        return pltpu.make_async_remote_copy(
            src_ref=sent.at[way, index],
            dst_ref=got.at[way, index],
            send_sem=send_sem.at[way, index],
            recv_sem=recv_sem.at[way, index],
            device_id=ring[way],
            device_id_type=MESH,
        )

    copies = [[message(way, index) for index in range(7)] for way in range(2)]
    for index in range(7):
        step = (index + 3) // 2
        first = index % 2 == 0
        for way in range(2):
            x_to = way if first else 1 - way
            z_to = (z + (5 - step)) % 8 if way == 0 else (z + 8 - (5 - step)) % 8

            def store(rows, total, way=way, index=index):
                sent[way, index, rows, :] = total

            term(x_to, z_to, store)
            if index == 0 and way == 0:
                pl.semaphore_wait(barrier, 3)
            if index >= 2:
                copies[way][index - 2].wait_recv()
                sent[way, index] += got[way, index - 2]
            copies[way][index].start()
    for x_to in range(2):

        def store(rows, total, x_to=x_to):
            mine[x_to, rows, :] = total

        term(x_to, z, store)
    for index in (5, 6):
        for way in range(2):
            copies[way][index].wait_recv()
    away = 1 - x
    side_sent[...] = mine[away] + (got[0, 6 - away] + got[1, 5 + away])
    last = pltpu.make_async_remote_copy(
        src_ref=side_sent,
        dst_ref=side_got,
        send_sem=send_sem.at[2, 0],
        recv_sem=recv_sem.at[2, 0],
        device_id=beside,
        device_id_type=MESH,
    )
    last.start()
    mine[x] += got[0, 6 - x] + got[1, 5 + x]
    last.wait_recv()
    out[...] = mine[x] + side_got[...]
    for way in range(2):
        for index in range(7):
            copies[way][index].wait_send()
    last.wait_send()


def vmem_specs(count):
    return [pl.BlockSpec(memory_space=pltpu.VMEM)] * count


ANY = pl.BlockSpec(memory_space=pl.ANY)


def local(sources, leaf_maps, mode_ids):
    planes, boxes, rhs, points = sources.shape
    face = points // 2
    square = jax.ShapeDtypeStruct((face, face), F32)
    rows = jax.ShapeDtypeStruct((rhs, face), F32)
    full = pltpu.VMEM((face, face), F32)
    short = pltpu.VMEM((face, face), BF16)
    left = pltpu.VMEM((face, 3 * face), BF16)
    right = pltpu.VMEM((3 * face, face), BF16)
    params = pltpu.CompilerParams(vmem_limit_bytes=VMEM_LIMIT)

    def cost(units, size):
        return pl.CostEstimate(
            flops=units * 2 * face**3, bytes_accessed=size * 4 * face**2, transcendentals=0
        )

    here = lax.axis_index("gz")
    other_sources = swapped(sources, "gz")
    o_33, o_31, near_gain, inv, through = pl.pallas_call(
        near_kernel,
        out_shape=[square] * 5,
        in_specs=[ANY],
        out_specs=vmem_specs(5),
        scratch_shapes=[full] * 6
        + [left, left, left, right, right, short, short, full, pltpu.SemaphoreType.DMA((6,))],
        compiler_params=params,
        cost_estimate=cost(30, 11),
        name="level_one_near",
    )(leaf_maps)
    y_33 = swapped(o_33, "box")
    y_32 = swapped(o_31, "box")
    core = here % 2
    modes = lax.dynamic_slice(mode_ids.reshape(-1, 2), (0, core), (16, 1)).reshape(16)
    lanes = jnp.arange(planes, dtype=jnp.int32)
    z_index = jnp.concatenate([here * planes + lanes, (here + 1 - 2 * core) * planes + lanes])
    cas = cas_table(modes, z_index, NZ).reshape(-1)
    lines = boxes * rhs
    line = (lines, points)
    spectral = pl.pallas_call(
        sums_kernel,
        out_shape=jax.ShapeDtypeStruct(line, F32),
        in_specs=[pl.BlockSpec(memory_space=pltpu.SMEM)] + vmem_specs(2),
        out_specs=vmem_specs(1)[0],
        scratch_shapes=[
            pltpu.VMEM((2, 7, *line), F32),
            pltpu.VMEM((2, 7, *line), F32),
            pltpu.VMEM((2, *line), F32),
            pltpu.VMEM(line, F32),
            pltpu.VMEM(line, F32),
            pltpu.SemaphoreType.DMA((3, 7)),
            pltpu.SemaphoreType.DMA((3, 7)),
        ],
        compiler_params=pltpu.CompilerParams(
            vmem_limit_bytes=VMEM_LIMIT, collective_id=0, has_side_effects=True
        ),
        cost_estimate=cost(100, 5),
        name="hartley_sums",
    )(cas, sources.reshape(planes, *line), other_sources.reshape(planes, *line))
    o_11, o_13, far_gain = pl.pallas_call(
        far_kernel,
        out_shape=[square] * 3,
        in_specs=[ANY] + vmem_specs(2),
        out_specs=vmem_specs(3),
        scratch_shapes=[full] * 5 + [left, right, right, pltpu.SemaphoreType.DMA((5,))],
        compiler_params=params,
        cost_estimate=cost(15, 10),
        name="level_one_far",
    )(leaf_maps, inv, through)
    near_data, far_data = pl.pallas_call(
        data_kernel,
        out_shape=[rows] * 2,
        in_specs=[ANY] + vmem_specs(3),
        out_specs=vmem_specs(2),
        scratch_shapes=[full] * 2 + [pltpu.SemaphoreType.DMA((2,))],
        compiler_params=params,
        cost_estimate=cost(2, 4),
        name="level_one_data",
    )(leaf_maps, spectral.reshape(boxes, rhs, points), near_gain, far_gain)
    other_data = swapped(near_data, "box")
    out, gain = pl.pallas_call(
        top_kernel,
        out_shape=[jax.ShapeDtypeStruct((face, points), F32), square],
        in_specs=vmem_specs(5),
        out_specs=[ANY] + vmem_specs(1),
        scratch_shapes=[full, full, left, left, right, right, short, short, full]
        + [pltpu.SemaphoreType.DMA],
        compiler_params=params,
        cost_estimate=cost(25, 8),
        name="level_two_gain",
    )(y_33, o_33, o_31, o_13, o_11)
    out, data = pl.pallas_call(
        last_kernel,
        out_shape=[jax.ShapeDtypeStruct((face, points), F32), rows],
        in_specs=vmem_specs(6) + [ANY],
        out_specs=[ANY] + vmem_specs(1),
        scratch_shapes=[full, left, right, pltpu.SemaphoreType.DMA],
        input_output_aliases={6: 0},
        compiler_params=params,
        cost_estimate=cost(4, 5),
        name="level_two_rows",
    )(y_32, gain, y_33, near_data, far_data, other_data, out)
    return (out[None, None], data[None, None])


def solution(mesh):
    placed = (P("gz", "box", None, None), P("gz", "box", None, None), P())
    return jax.shard_map(
        local,
        mesh=mesh,
        in_specs=placed,
        out_specs=(P("gz", "box", None, None), P("gz", "box", None, None)),
        check_vma=False,
    )
```

time: 171 us -> 90.3 us (0.53)
  matrix products: 97.3 us -> 0 us
  Pallas kernels: 0 us -> 77.3 us
  other arithmetic: 26.8 us -> 0.21 us
  between operations: 14.3 us -> 0.96 us
  local copies, waits for them, and re-layouts: 13.7 us -> 4.73 us
  loops' own time: 8.54 us -> 0 us
  waiting for transfers between devices: 4.44 us -> 0.01 us
    dot_general x36 -> x0, matrix products: 97.3 us -> none  [the longest x29 84.3 us: mul(): jnp.dot(left_mat, right_mat, precision=lax.Precision.HIGH, preferred_elem...]
    pallas_call x0 -> x6, Pallas kernels: none -> 77.3 us  [the longest x1 33.5 us: local(): pl.pallas_call(sums_kernel, out_shape=jax.ShapeDtypeStruct(line, F32), in...]
    reduce_sum x12 -> x0, other arithmetic: 25.3 us -> none  [step(): return (count + 1, total, power, jnp.sum(power * power))]
    another operation x2 -> x0, loops' own time: 8.54 us -> none  [inverse(): lax.while_loop(again, step, (0, total, power, jnp.sum(power * power)))]
    dynamic_slice x2 -> x1, local copies, waits for them, and re-layouts: 4.88 us -> 0.19 us  [local(): lax.dynamic_slice(mode_ids.reshape(-1, 2), (0, core), (16, 1)).reshape(16)]
    ppermute x3 -> x4, waiting for transfers between devices: 4.43 us -> 0.01 us  [swapped(): return lax.ppermute(block, axis, route)]
    dot_general x1 -> x0, local copies, waits for them, and re-layouts: 4.38 us -> none  [local(): jnp.einsum('mz,zbrp->mbrp', cas_rows, sources, precision=lax.Precision.HIGH)]
    ppermute x3 -> x4, starting transfers between devices: 4.28 us -> 5.46 us  [swapped(): return lax.ppermute(block, axis, route)]
  transfers between devices with their start and end apart: 4 -> 4, of which waited for: 1 -> 0; matrix products, arithmetic and copies ran while one was open for 72% -> 1% of each run, Pallas kernels for 0% -> 84%
where the time goes in v2:
time: 90.3 us; the launch traced here: 88.6 us
  Pallas kernels  77.3 us (86%)
  starting transfers between devices  5.46 us (6%)
  local copies, waits for them, and re-layouts  4.73 us (5%)
  between operations  0.96 us (1%)
    pallas_call x1, Pallas kernels, local(): pl.pallas_call(sums_kernel, out_shape=jax.ShapeDtypeStruct(line, F32), in...  33.5 us
    pallas_call x1, Pallas kernels, local(): pl.pallas_call(top_kernel, out_shape=[jax.ShapeDtypeStruct((face, points)...  16.1 us
    pallas_call x1, Pallas kernels, local(): pl.pallas_call(near_kernel, out_shape=[square] * 5, in_specs=[ANY], out_s...  14.7 us
    pallas_call x1, Pallas kernels, local(): pl.pallas_call(far_kernel, out_shape=[square] * 3, in_specs=[ANY] + vmem_...  6.84 us
    ppermute x4, starting transfers between devices, swapped(): return lax.ppermute(block, axis, route)  5.46 us
    unnamed x12, local copies, waits for them, and re-layouts  4.38 us
    pallas_call x1, Pallas kernels, local(): pl.pallas_call(data_kernel, out_shape=[rows] * 2, in_specs=[ANY] + vmem_s...  3.17 us
    pallas_call x1, Pallas kernels, local(): pl.pallas_call(last_kernel, out_shape=[jax.ShapeDtypeStruct((face, points...  3 us
  transfers between devices with their start and end apart: 4, of which 0 were waited for; matrix products, arithmetic and copies ran while one was open for 1% of the time, Pallas kernels for 84%

profile of v2, /device:TPU:8, one launch (start us, length us, event | category | flops | bytes accessed | tf_op | source)
XLA Modules:
  0.0 88.6 jit_solution(2548565802310026990)
XLA Ops:
  0.6 0.0 copy-start.5
  0.6 0.1 collective-permute-start.2
  0.7 14.7 %level_one_near.1 = (f32[512,512]{1,0:T(8,128)}, f32[512,512]{1,0:T(8,128)}, f32[512,512]{1,0:T(8,128)S(1)}, f32[512,512]{1,0:T(8,128)S(1)}, f32[512,512]{1,0:T(8,128)S(1)}) custom-call(f32[1,2,1024,1024]{3,2,1,0:T(8,128)} %maps.5), custom_call_target="tpu_custom_call" | custom-call | flops 8053063680 | bytes 11534336 | tf_op jit(solution)/shard_map/level_one_near/pallas_call | solution.py:485
  15.5 0.0 copy-start.1
  15.5 1.0 %copy-done.1 = f32[512,512]{1,0:T(8,128)} copy-done((f32[512,512]{1,0:T(8,128)}, f32[512,512]{1,0:T(8,128)S(1)}, u32[]{:S(2)}) %copy-start.1) | copy-done | bytes 1048600
  16.5 0.0 copy-start.3
  16.5 1.0 %copy-done.3 = f32[512,512]{1,0:T(8,128)} copy-done((f32[512,512]{1,0:T(8,128)}, f32[512,512]{1,0:T(8,128)S(1)}, u32[]{:S(2)}) %copy-start.3) | copy-done | bytes 1048600
  17.4 4.8 %collective-permute-start.1 = (f32[512,512]{1,0:T(8,128)}, f32[512,512]{1,0:T(8,128)S(1)}, u32[]{:S(2)}, u32[]{:S(2)}) collective-permute-start(f32[512,512]{1,0:T(8,128)} %get-tuple-element.17.o_33), channel_id=1, source_target_pairs={{0,1},{1,0},{2,3},{3,2},{4,5},{5,4},{6,7},{7,6},{8,9},{9,8},{10,11... | collective-permute-start | bytes 3145736 | tf_op jit(solution)/shard_map/ppermute | solution.py:23
  22.2 0.0 collective-permute-start
  22.3 0.0 copy-done.5
  22.3 0.1 reshape.21
  22.3 0.2 dynamic-slice_reduce_fusion
  22.5 0.1 pad_add_fusion
  22.6 0.1 broadcast_multiply_fusion
  22.7 0.1 mul.42
  22.8 0.1 add_multiply_fusion.cas
  22.8 0.0 copy-start.2
  22.8 1.2 %copy-done.2 = f32[512,512]{1,0:T(8,128)S(1)} copy-done((f32[512,512]{1,0:T(8,128)S(1)}, f32[512,512]{1,0:T(8,128)}, u32[]{:S(2)}) %copy-start.2) | copy-done | bytes 1048600
  24.1 0.0 copy-start.4
  24.1 1.2 %copy-done.4 = f32[512,512]{1,0:T(8,128)S(1)} copy-done((f32[512,512]{1,0:T(8,128)S(1)}, f32[512,512]{1,0:T(8,128)}, u32[]{:S(2)}) %copy-start.4) | copy-done | bytes 1048600
  25.3 0.0 copy-start
  25.3 6.8 %level_one_far.1 = (f32[512,512]{1,0:T(8,128)S(1)}, f32[512,512]{1,0:T(8,128)S(1)}, f32[512,512]{1,0:T(8,128)S(1)}) custom-call(f32[1,2,1024,1024]{3,2,1,0:T(8,128)} %maps.5, f32[512,512]{1,0:T(8,128)S(1)} %copy-done.2, f32[512,512]{1,0:T(8,128)S(1)} %copy-done.4), custom_call_target="tpu_custom_call" | custom-call | flops 4026531840 | bytes 10485760 | tf_op jit(solution)/shard_map/level_one_far/pallas_call | solution.py:525
  32.1 0.0 collective-permute-done.2
  32.1 0.0 copy-done
  32.2 33.5 %hartley_sums.1 = f32[32,1024]{1,0:T(8,128)S(1)} custom-call(f32[512]{0:T(512)S(1)} %add_multiply_fusion.cas, f32[16,32,1024]{2,1,0:T(8,128)S(1)} %bitcast.6, f32[16,32,1024]{2,1,0:T(8,128)} %bitcast.1.other), custom_call_target="tpu_custom_call" | custom-call | flops 26843545600 | bytes 5242880 | tf_op jit(solution)/shard_map/hartley_sums/pallas_call | solution.py:505
  65.6 3.2 %level_one_data.1 = (f32[16,512]{1,0:T(8,128)S(1)}, f32[16,512]{1,0:T(8,128)S(1)}) custom-call(f32[1,2,1024,1024]{3,2,1,0:T(8,128)} %maps.5, f32[2,16,1024]{2,1,0:T(8,128)S(1)} %bitcast.5, f32[512,512]{1,0:T(8,128)S(1)} %get-tuple-element.23.near_gain, f32[512,512]{1,0:T(8,128)S(1)} %get-tuple-element.24.far_gain), custom_call_target="tpu_custom_call" | custom-call | flops 536870912 | bytes 4194304 | tf_op jit(solution)/shard_map/level_one_data/pallas_call | solution.py:535
  68.8 0.5 collective-permute-start.3
  69.3 0.0 collective-permute-done.1.y_33
  69.3 16.1 %level_two_gain.1 = (f32[512,1024]{1,0:T(8,128)}, f32[512,512]{1,0:T(8,128)S(1)}) custom-call(f32[512,512]{1,0:T(8,128)S(1)} %collective-permute-done.1.y_33, f32[512,512]{1,0:T(8,128)} %get-tuple-element.17.o_33, f32[512,512]{1,0:T(8,128)} %get-tuple-element.16.o_31, f32[512,512]{1,0:T(8,128)S(1)} %get-tuple-element.20.o_13, ...), custom_call_target="tpu_custom_call" | custom-call | flops 6710886400 | bytes 8388608 | tf_op jit(solution)/shard_map/level_two_gain/pallas_call | solution.py:546
  85.4 0.0 collective-permute-done.y_32
  85.4 0.0 collective-permute-done.3.other_data
  85.4 3.0 %level_two_rows.1 = (f32[512,1024]{1,0:T(8,128)}, f32[16,512]{1,0:T(8,128)}) custom-call(f32[512,512]{1,0:T(8,128)S(1)} %collective-permute-done.y_32, f32[512,512]{1,0:T(8,128)S(1)} %get-tuple-element.22.gain, f32[512,512]{1,0:T(8,128)S(1)} %collective-permute-done.1.y_33, ...), custom_call_target="tpu_custom_call", output_to_operand_aliasing={{0}: (6, {})} | custom-call | flops 1073741824 | bytes 5242880 | tf_op jit(solution)/shard_map/level_two_rows/pallas_call | solution.py:557
  (1 shorter events, 0.0 us)
Async XLA Ops:
  0.6 21.6 %copy-start.5 = (s32[32]{0:T(128)S(1)}, s32[32]{0:T(128)}, u32[]{:S(2)}) copy-start(s32[32]{0:T(128)} %param.5) | copy-start | bytes 388
  0.6 31.5 %collective-permute-start.2 = (f32[16,2,16,1024]{3,2,1,0:T(8,128)}, f32[16,2,16,1024]{3,2,1,0:T(8,128)}, u32[]{:S(2)}, u32[]{:S(2)}) collective-permute-start(f32[16,2,16,1024]{3,2,1,0:T(8,128)} %param.3), channel_id=1, source_target_pairs={{0,8},{8,0},{16,24},{24,16},{32,40},{40,32},{48,56},{56,48},{64,72... | collective-permute-start | bytes 6291464 | tf_op jit(solution)/shard_map/ppermute | solution.py:23
  15.5 1.0 %copy-start.1 = (f32[512,512]{1,0:T(8,128)}, f32[512,512]{1,0:T(8,128)S(1)}, u32[]{:S(2)}) copy-start(f32[512,512]{1,0:T(8,128)S(1)} %get-tuple-element.18.inv) | copy-start | bytes 3145732
  16.5 1.0 %copy-start.3 = (f32[512,512]{1,0:T(8,128)}, f32[512,512]{1,0:T(8,128)S(1)}, u32[]{:S(2)}) copy-start(f32[512,512]{1,0:T(8,128)S(1)} %get-tuple-element.19.through) | copy-start | bytes 3145732
  17.4 51.9 %collective-permute-start.1 = (f32[512,512]{1,0:T(8,128)}, f32[512,512]{1,0:T(8,128)S(1)}, u32[]{:S(2)}, u32[]{:S(2)}) collective-permute-start(f32[512,512]{1,0:T(8,128)} %get-tuple-element.17.o_33), channel_id=1, source_target_pairs={{0,1},{1,0},{2,3},{3,2},{4,5},{5,4},{6,7},{7,6},{8,9},{9,8},{10,11... | collective-permute-start | bytes 3145736 | tf_op jit(solution)/shard_map/ppermute | solution.py:23
  22.2 63.2 %collective-permute-start = (f32[512,512]{1,0:T(8,128)}, f32[512,512]{1,0:T(8,128)S(1)}, u32[]{:S(2)}, u32[]{:S(2)}) collective-permute-start(f32[512,512]{1,0:T(8,128)} %get-tuple-element.16.o_31), channel_id=1, source_target_pairs={{0,1},{1,0},{2,3},{3,2},{4,5},{5,4},{6,7},{7,6},{8,9},{9,8},{10,11... | collective-permute-start | bytes 3145736 | tf_op jit(solution)/shard_map/ppermute | solution.py:23
  22.8 1.2 %copy-start.2 = (f32[512,512]{1,0:T(8,128)S(1)}, f32[512,512]{1,0:T(8,128)}, u32[]{:S(2)}) copy-start(f32[512,512]{1,0:T(8,128)} %copy-done.1) | copy-start | bytes 3145732
  24.1 1.2 %copy-start.4 = (f32[512,512]{1,0:T(8,128)S(1)}, f32[512,512]{1,0:T(8,128)}, u32[]{:S(2)}) copy-start(f32[512,512]{1,0:T(8,128)} %copy-done.3) | copy-start | bytes 3145732
  25.3 6.9 %copy-start = (f32[16,2,16,1024]{3,2,1,0:T(8,128)S(1)}, f32[16,2,16,1024]{3,2,1,0:T(8,128)}, u32[]{:S(2)}) copy-start(f32[16,2,16,1024]{3,2,1,0:T(8,128)} %param.3) | copy-start | bytes 6291460
  68.8 16.6 %collective-permute-start.3 = (f32[16,512]{1,0:T(8,128)S(1)}, f32[16,512]{1,0:T(8,128)S(1)}, u32[]{:S(2)}, u32[]{:S(2)}) collective-permute-start(f32[16,512]{1,0:T(8,128)S(1)} %get-tuple-element.25.near_data), channel_id=1, source_target_pairs={{0,1},{1,0},{2,3},{3,2},{4,5},{5,4},{6,7},{7,6},{8,9},{9,8},{10,11... | collective-permute-start | bytes 98312 | tf_op jit(solution)/shard_map/ppermute | solution.py:23

commit v3 on v2

v3 whole, which is shorter than its diff:
```python
import jax
import jax.numpy as jnp
from jax import lax
from jax.experimental import pallas as pl
from jax.experimental.pallas import tpu as pltpu
from jax.sharding import PartitionSpec as P

NZ = 512
MESH = pl.DeviceIdType.MESH
F32 = jnp.float32
BF16 = jnp.bfloat16
HALF = 256
FINE = 3.6e-9
VMEM_LIMIT = 60 * 1024 * 1024
LESS_VMEM = 50 * 1024 * 1024
LAST_VMEM = 28 * 1024 * 1024


def swapped(block, axis):
    count = lax.axis_size(axis)
    route = []
    for low in range(0, count, 2):
        route += [(low, low + 1), (low + 1, low)]
    return lax.ppermute(block, axis, route)


def cas_table(mode_list, z_index, length_z):
    phase = mode_list[:, None] * z_index[None, :] % length_z
    angle = phase.astype(F32) * (2.0 * jnp.pi / length_z)
    return (jnp.cos(angle) + jnp.sin(angle)) / jnp.sqrt(jnp.float32(length_z))


def split(value):
    high = value.astype(BF16)
    return high, (value - high.astype(F32)).astype(BF16)


def put_left(ref, start, value):
    face = value.shape[1]
    high, low = split(value)
    rows = pl.ds(start, value.shape[0])
    ref[rows, 0:face] = high
    ref[rows, face : 2 * face] = high
    ref[rows, 2 * face : 3 * face] = low


def put_right(ref, start, value):
    face = ref.shape[0] // 3
    high, low = split(value)
    count = value.shape[0]
    ref[pl.ds(start, count), :] = high
    ref[pl.ds(face + start, count), :] = low
    ref[pl.ds(2 * face + start, count), :] = high


def fill(put, ref, source):
    for start in range(0, source.shape[0], HALF):
        put(ref, start, source[start : start + HALF, :])


def product(left, right, start):
    return jnp.dot(left[start : start + HALF, :], right[...], preferred_element_type=F32)


def halves(face):
    return range(0, face, HALF)


def eye_rows(start, face):
    row = lax.broadcasted_iota(jnp.int32, (HALF, face), 0) + start
    col = lax.broadcasted_iota(jnp.int32, (HALF, face), 1)
    return jnp.where(row == col, 1.0, 0.0).astype(F32)


def chunk_sum(part):
    return jnp.sum(part.reshape(-1, 8, part.shape[1]), axis=0)


def invert(k_left, total, power, rough, left, right, spare):
    face = total.shape[0]

    def raise_power():
        parts = [
            jnp.dot(power[s : s + HALF, :], power[...], preferred_element_type=F32)
            for s in halves(face)
        ]
        for s, part in zip(halves(face), parts):
            power[s : s + HALF, :] = part.astype(BF16)

    def gather():
        for s in halves(face):
            rough[s : s + HALF, :] = total[s : s + HALF, :].astype(BF16)
        for s in halves(face):
            total[s : s + HALF, :] += jnp.dot(
                rough[s : s + HALF, :], power[...], preferred_element_type=F32
            )

    raise_power()
    for _ in range(3):
        gather()
        raise_power()
    gather()
    for s in halves(face):
        rough[s : s + HALF, :] = total[s : s + HALF, :].astype(BF16)
    first = jnp.zeros((8, face), F32)
    for s in halves(face):
        part = jnp.dot(
            k_left[s : s + HALF, 0:face], rough[...], preferred_element_type=F32
        ) + jnp.dot(
            k_left[s : s + HALF, 2 * face : 3 * face], rough[...], preferred_element_type=F32
        )
        part = part - rough[s : s + HALF, :].astype(F32) + eye_rows(s, face)
        spare[s : s + HALF, :] = part
        power[s : s + HALF, :] = part.astype(BF16)
        first += chunk_sum(part * part)
    second = jnp.zeros((8, face), F32)
    for s in halves(face):
        part = jnp.dot(power[s : s + HALF, :], power[...], preferred_element_type=F32)
        second += chunk_sum(part * part)
        spare[s : s + HALF, :] += part
    for s in halves(face):
        power[s : s + HALF, :] = spare[s : s + HALF, :].astype(BF16)
    for s in halves(face):
        total[s : s + HALF, :] = rough[s : s + HALF, :].astype(F32) + jnp.dot(
            rough[s : s + HALF, :], power[...], preferred_element_type=F32
        )
    first, second = jnp.sum(first), jnp.sum(second)

    @pl.when(jnp.logical_not((first < 0.25) & (first * second < FINE)))
    def _():
        careful(k_left, total, left, right, spare)


def careful(k_left, total, left, right, spare):
    face = total.shape[0]
    for s in halves(face):
        kept = k_left[s : s + HALF, 0:face].astype(F32)
        kept += k_left[s : s + HALF, 2 * face : 3 * face].astype(F32)
        spare[s : s + HALF, :] = kept
        total[s : s + HALF, :] = kept + eye_rows(s, face)

    def raise_power():
        fill(put_left, left, spare)
        fill(put_right, right, spare)
        size = 0.0
        for s in halves(face):
            part = product(left, right, s)
            spare[s : s + HALF, :] = part
            size += jnp.sum(part * part)
        return size

    def squaring(state):
        count, _ = state
        fill(put_left, left, total)
        fill(put_right, right, spare)
        for s in halves(face):
            total[s : s + HALF, :] += product(left, right, s)
        return count + 1, raise_power()

    lax.while_loop(
        lambda state: (state[1] > 1e-15) & (state[0] < 48),
        squaring,
        (jnp.int32(0), raise_power()),
    )

    def newton(state):
        count, last, _ = state
        fill(put_right, right, total)
        size = 0.0
        for s in halves(face):
            part = product(k_left, right, s) - total[s : s + HALF, :] + eye_rows(s, face)
            spare[s : s + HALF, :] = part
            size += jnp.sum(part * part)
        better = size < 0.25 * last

        @pl.when(better)
        def _():
            fill(put_left, left, total)
            fill(put_right, right, spare)
            for s in halves(face):
                total[s : s + HALF, :] += product(left, right, s)

        return count + 1, size, better

    lax.while_loop(
        lambda state: state[2] & (state[0] < 4),
        newton,
        (jnp.int32(0), jnp.float32(1.0), jnp.bool_(True)),
    )


def fetcher(maps, sems, face):
    def fetch(slot, leaf, row, col, dst):
        copy = pltpu.make_async_copy(
            maps.at[
                0,
                leaf,
                pl.ds(pl.multiple_of(row * face, face), face),
                pl.ds(pl.multiple_of(col * face, face), face),
            ],
            dst,
            sems.at[slot],
        )
        copy.start()
        return copy

    return fetch


def started(src, dst, sem):
    copy = pltpu.make_async_copy(src, dst, sem)
    copy.start()
    return copy


def near_kernel(maps, o_33_out, o_31_out, gain_out, inv_out, through_out, *scratch):
    a_33, b_33, b_32, b_23, b_22, a_31, gain, inv, through = scratch[:9]
    l_one, l_two, k_left, r_one, r_two, power, rough, spare, sems = scratch[9:]
    face = a_33.shape[0]
    far = lax.axis_index("box") % 2
    near = 1 - far
    fetch = fetcher(maps, sems, face)
    copies = [
        fetch(0, far, near, near, a_33),
        fetch(1, near, far, far, b_33),
        fetch(2, near, far, near, b_32),
        fetch(3, near, near, far, b_23),
        fetch(4, near, near, near, b_22),
        fetch(5, far, near, far, a_31),
    ]
    copies[0].wait()
    fill(put_left, l_one, a_33)
    copies[1].wait()
    fill(put_right, r_one, b_33)
    for s in halves(face):
        part = product(l_one, r_one, s)
        put_left(k_left, s, part)
        power[s : s + HALF, :] = part.astype(BF16)
        inv[s : s + HALF, :] = part + eye_rows(s, face)
    copies[2].wait()
    fill(put_right, r_one, b_32)
    for s in halves(face):
        part = product(l_one, r_one, s)
        through[s : s + HALF, :] = part
        put_right(r_two, s, part)
    outs = [started(through, through_out, sems.at[6])]
    invert(k_left, inv, power, rough, l_one, r_one, spare)
    outs.append(started(inv, inv_out, sems.at[7]))
    copies[3].wait()
    fill(put_left, l_one, b_23)
    fill(put_right, r_one, inv)
    for s in halves(face):
        part = product(l_one, r_one, s)
        gain[s : s + HALF, :] = part
        put_left(l_two, s, part)
    outs.append(started(gain, gain_out, sems.at[8]))
    copies[4].wait()
    for s in halves(face):
        b_22[s : s + HALF, :] += product(l_two, r_two, s)
    outs.append(started(b_22, o_33_out, sems.at[9]))
    copies[5].wait()
    fill(put_right, r_one, a_31)
    for s in halves(face):
        a_31[s : s + HALF, :] = -product(l_two, r_one, s)
    outs.append(started(a_31, o_31_out, sems.at[10]))
    for copy in outs:
        copy.wait()


def keep_pair(highs, lows, start, value):
    high, low = split(value)
    highs[start : start + value.shape[0], :] = high
    lows[start : start + value.shape[0], :] = low


def rows_times(rows, highs, lows):
    r_high, r_low = split(rows)

    def dot(left, right):
        return lax.dot_general(
            left, right, (((1,), (1,)), ((), ())), preferred_element_type=F32
        )

    return dot(r_high, highs[...]) + (dot(r_low, highs[...]) + dot(r_high, lows[...]))


def top_kernel(y_33_in, o_33_in, o_31_in, o_13_in, o_11_in, out, gain_out, *scratch):
    y_33, o_33, o_31, o_13, o_11, gain, inv = scratch[:7]
    l_one, k_left, r_one, r_two, power, rough, spare, sems = scratch[7:]
    face = y_33.shape[0]
    far = lax.axis_index("box") % 2
    copies = [
        started(src, dst, sems.at[slot])
        for slot, (src, dst) in enumerate(
            (
                (y_33_in, y_33),
                (o_33_in, o_33),
                (o_31_in, o_31),
                (o_13_in, o_13),
                (o_11_in, o_11),
            )
        )
    ]
    copies[0].wait()
    fill(put_left, l_one, y_33)
    copies[1].wait()
    fill(put_right, r_one, o_33)
    for s in halves(face):
        part = product(l_one, r_one, s)
        put_left(k_left, s, part)
        power[s : s + HALF, :] = part.astype(BF16)
        inv[s : s + HALF, :] = part + eye_rows(s, face)
    copies[2].wait()
    fill(put_right, r_one, o_31)
    for s in halves(face):
        put_right(r_two, s, product(l_one, r_one, s))
    invert(k_left, inv, power, rough, l_one, r_one, spare)
    copies[3].wait()
    fill(put_left, l_one, o_13)
    fill(put_right, r_one, inv)
    for s in halves(face):
        part = product(l_one, r_one, s)
        gain[s : s + HALF, :] = part
        put_left(k_left, s, part)
    last = [started(gain, gain_out, sems.at[5])]
    scale = (2.0 * face) ** 0.5
    copies[4].wait()
    for s in halves(face):
        o_11[s : s + HALF, :] = (o_11[s : s + HALF, :] + product(k_left, r_two, s)) * scale
        last.append(
            started(
                o_11.at[s : s + HALF, :],
                out.at[s : s + HALF, pl.ds(pl.multiple_of(far * face, face), face)],
                sems.at[6 + s // HALF],
            )
        )
    for copy in last:
        copy.wait()


def last_kernel(
    y_32, gain, y_33, near_data, far_data, other_data, _, out, data, other, left, right, sems
):
    face = gain.shape[0]
    near = 1 - lax.axis_index("box") % 2
    scale = (2.0 * face) ** 0.5
    fill(put_left, left, gain)
    fill(put_right, right, y_32)
    copies = []
    for s in halves(face):
        other[s : s + HALF, :] = product(left, right, s) * -scale
        copies.append(
            started(
                other.at[s : s + HALF, :],
                out.at[s : s + HALF, pl.ds(pl.multiple_of(near * face, face), face)],
                sems.at[s // HALF],
            )
        )
    jump = rows_times(near_data[...], *split(y_33[...])) - other_data[...]
    data[...] = far_data[...] + rows_times(jump, *split(gain[...]))
    for copy in copies:
        copy.wait()


def sums_kernel(
    cas, own_in, other_in, maps, inv_in, through_in, near_gain_in, o_11_out, o_13_out, *scratch
):
    near_data, far_data, sent, got, mine, side_sent, side_got, send_sem, recv_sem = scratch[:9]
    a_13, b_33, b_32, a_11, a_31, a_33, inv, through, near_gain, gain, o_13 = scratch[9:20]
    left, r_one, r_two, near_high, near_low, far_high, far_low, own, other, sems = scratch[20:]
    face = inv.shape[0]
    far = lax.axis_index("box") % 2
    near = 1 - far
    fetch = fetcher(maps, sems, face)
    planes_in = (started(own_in, own, sems.at[11]), started(other_in, other, sems.at[12]))
    copies_in = [
        fetch(0, far, far, near, a_13),
        fetch(1, near, far, far, b_33),
        fetch(2, near, far, near, b_32),
        started(inv_in, inv, sems.at[3]),
        fetch(4, far, near, far, a_31),
        fetch(5, far, far, far, a_11),
        started(through_in, through, sems.at[6]),
        fetch(7, far, near, near, a_33),
        started(near_gain_in, near_gain, sems.at[8]),
    ]
    planes = own.shape[0]
    here = lax.axis_index("gz")
    core, z, x = here % 2, here // 2 % 8, here // 16

    def device(x_at, z_at):
        return {"gz": x_at * 16 + z_at * 2 + core}

    ring = (device(x, (z + 1) % 8), device(x, (z + 7) % 8))
    beside = device(1 - x, z)
    barrier = pltpu.get_barrier_semaphore()
    for target in (*ring, beside):
        pl.semaphore_signal(barrier, inc=1, device_id=target, device_id_type=MESH)
    for copy in planes_in:
        copy.wait()

    def term(x_to, z_to, store):
        row = (x_to * 8 + z_to) * (2 * planes)

        def block(part, carry):
            rows = pl.ds(pl.multiple_of(part * 8, 8), 8)
            total = cas[row] * own[0, rows, :]
            for k in range(1, planes):
                total += cas[row + k] * own[k, rows, :]
            for k in range(planes):
                total += cas[row + planes + k] * other[k, rows, :]
            store(rows, total)
            return carry

        lax.fori_loop(0, own.shape[1] // 8, block, 0)

    def message(way, index):
        return pltpu.make_async_remote_copy(
            src_ref=sent.at[way, index],
            dst_ref=got.at[way, index],
            send_sem=send_sem.at[way, index],
            recv_sem=recv_sem.at[way, index],
            device_id=ring[way],
            device_id_type=MESH,
        )

    copies_out = []

    def work_0():
        copies_in[0].wait()
        fill(put_left, left, a_13)
        copies_in[1].wait()
        fill(put_right, r_one, b_33)
        for s in halves(face):
            gain[s : s + HALF, :] = product(left, r_one, s)

    def work_1():
        copies_in[2].wait()
        fill(put_right, r_two, b_32)
        for s in halves(face):
            o_13[s : s + HALF, :] = -product(left, r_two, s)

    def work_2():
        copies_in[3].wait()
        fill(put_left, left, gain)
        fill(put_right, r_one, inv)
        for s in halves(face):
            gain[s : s + HALF, :] = product(left, r_one, s)

    def work_3():
        fill(put_left, left, gain)
        copies_in[4].wait()
        copies_in[5].wait()
        fill(put_right, r_one, a_31)
        for s in halves(face):
            a_11[s : s + HALF, :] += product(left, r_one, s)
        copies_out.append(started(a_11, o_11_out, sems.at[9]))

    def work_4():
        copies_in[6].wait()
        fill(put_right, r_two, through)
        for s in halves(face):
            o_13[s : s + HALF, :] -= product(left, r_two, s)
        copies_out.append(started(o_13, o_13_out, sems.at[10]))

    def work_5():
        copies_in[7].wait()
        copies_in[8].wait()
        for s in halves(face):
            rows = slice(s, s + HALF)
            keep_pair(far_high, far_low, s, a_33[rows, :])
            keep_pair(far_high, far_low, face + s, a_13[rows, :])
            keep_pair(near_high, near_low, s, near_gain[rows, :])
            keep_pair(near_high, near_low, face + s, gain[rows, :])

    work = (work_0, work_1, work_2, work_3, work_4, work_5, lambda: None)
    copies = [[message(way, index) for index in range(7)] for way in range(2)]
    for index in range(7):
        step = (index + 3) // 2
        first = index % 2 == 0
        for way in range(2):
            x_to = way if first else 1 - way
            z_to = (z + (5 - step)) % 8 if way == 0 else (z + 8 - (5 - step)) % 8

            def store(rows, total, way=way, index=index):
                sent[way, index, rows, :] = total

            term(x_to, z_to, store)
            if index == 0 and way == 0:
                pl.semaphore_wait(barrier, 3)
            if index >= 2:
                copies[way][index - 2].wait_recv()
                sent[way, index] += got[way, index - 2]
            copies[way][index].start()
        work[index]()
    for x_to in range(2):

        def store(rows, total, x_to=x_to):
            mine[x_to, rows, :] = total

        term(x_to, z, store)
    for index in (5, 6):
        for way in range(2):
            copies[way][index].wait_recv()
    away = 1 - x
    side_sent[...] = mine[away] + (got[0, 6 - away] + got[1, 5 + away])
    last = pltpu.make_async_remote_copy(
        src_ref=side_sent,
        dst_ref=side_got,
        send_sem=send_sem.at[2, 0],
        recv_sem=recv_sem.at[2, 0],
        device_id=beside,
        device_id_type=MESH,
    )
    last.start()
    mine[x] += got[0, 6 - x] + got[1, 5 + x]
    last.wait_recv()
    mine[x] += side_got[...]
    rhs = near_data.shape[0]

    def info(leaf, side):
        return mine[
            x,
            pl.ds(pl.multiple_of(leaf * rhs, rhs), rhs),
            pl.ds(pl.multiple_of(side * face, face), face),
        ]

    known = rows_times(info(near, far), far_high, far_low)
    jump = info(far, near) - known[:, 0:face]
    moved = rows_times(jump, near_high, near_low)
    near_data[...] = info(near, near) - moved[:, 0:face]
    far_data[...] = info(far, far) + moved[:, face : 2 * face] - known[:, face : 2 * face]
    for way in range(2):
        for index in range(7):
            copies[way][index].wait_send()
    last.wait_send()
    for copy in copies_out:
        copy.wait()


def vmem_specs(count):
    return [pl.BlockSpec(memory_space=pltpu.VMEM)] * count


ANY = pl.BlockSpec(memory_space=pl.ANY)


def local(sources, leaf_maps, mode_ids):
    planes, boxes, rhs, points = sources.shape
    face = points // 2
    square = jax.ShapeDtypeStruct((face, face), F32)
    rows = jax.ShapeDtypeStruct((rhs, face), F32)
    full = pltpu.VMEM((face, face), F32)
    short = pltpu.VMEM((face, face), BF16)
    left = pltpu.VMEM((face, 3 * face), BF16)
    right = pltpu.VMEM((3 * face, face), BF16)
    params = pltpu.CompilerParams(vmem_limit_bytes=VMEM_LIMIT)

    def cost(units, size):
        return pl.CostEstimate(
            flops=units * 2 * face**3, bytes_accessed=size * 4 * face**2, transcendentals=0
        )

    here = lax.axis_index("gz")
    other_sources = swapped(sources, "gz")
    o_33, o_31, near_gain, inv, through = pl.pallas_call(
        near_kernel,
        out_shape=[square] * 5,
        in_specs=[ANY],
        out_specs=[ANY] * 5,
        scratch_shapes=[full] * 9
        + [left, left, left, right, right, short, short, full, pltpu.SemaphoreType.DMA((11,))],
        compiler_params=params,
        cost_estimate=cost(27, 11),
        name="level_one_near",
    )(leaf_maps)
    y_33 = swapped(o_33, "box")
    y_32 = swapped(o_31, "box")
    core = here % 2
    modes = lax.dynamic_slice(mode_ids.reshape(-1, 2), (0, core), (16, 1)).reshape(16)
    lanes = jnp.arange(planes, dtype=jnp.int32)
    z_index = jnp.concatenate([here * planes + lanes, (here + 1 - 2 * core) * planes + lanes])
    cas = cas_table(modes, z_index, NZ).reshape(-1)
    line = (boxes * rhs, points)
    pair = pltpu.VMEM((2 * face, face), BF16)
    o_11, o_13, near_data, far_data = pl.pallas_call(
        sums_kernel,
        out_shape=[square, square, rows, rows],
        in_specs=[pl.BlockSpec(memory_space=pltpu.SMEM)] + [ANY] * 6,
        out_specs=[ANY] * 2 + vmem_specs(2),
        scratch_shapes=[
            pltpu.VMEM((2, 7, *line), F32),
            pltpu.VMEM((2, 7, *line), F32),
            pltpu.VMEM((2, *line), F32),
            pltpu.VMEM(line, F32),
            pltpu.VMEM(line, F32),
            pltpu.SemaphoreType.DMA((3, 7)),
            pltpu.SemaphoreType.DMA((3, 7)),
        ]
        + [full] * 11
        + [left, right, right, pair, pair, pair, pair]
        + [pltpu.VMEM((planes, *line), F32)] * 2
        + [pltpu.SemaphoreType.DMA((13,))],
        compiler_params=pltpu.CompilerParams(
            vmem_limit_bytes=VMEM_LIMIT, collective_id=0, has_side_effects=True
        ),
        cost_estimate=cost(100, 5),
        name="hartley_sums",
    )(
        cas,
        sources.reshape(planes, *line),
        other_sources.reshape(planes, *line),
        leaf_maps,
        inv,
        through,
        near_gain,
    )
    other_data = swapped(near_data, "box")
    out, gain = pl.pallas_call(
        top_kernel,
        out_shape=[jax.ShapeDtypeStruct((face, points), F32), square],
        in_specs=[ANY] * 5,
        out_specs=[ANY] * 2,
        scratch_shapes=[full] * 7
        + [left, left, right, right, short, short, full, pltpu.SemaphoreType.DMA((8,))],
        compiler_params=pltpu.CompilerParams(vmem_limit_bytes=LESS_VMEM),
        cost_estimate=cost(22, 8),
        name="level_two_gain",
    )(y_33, o_33, o_31, o_13, o_11)
    out, data = pl.pallas_call(
        last_kernel,
        out_shape=[jax.ShapeDtypeStruct((face, points), F32), rows],
        in_specs=vmem_specs(6) + [ANY],
        out_specs=[ANY] + vmem_specs(1),
        scratch_shapes=[full, left, right, pltpu.SemaphoreType.DMA((2,))],
        input_output_aliases={6: 0},
        compiler_params=pltpu.CompilerParams(vmem_limit_bytes=LAST_VMEM),
        cost_estimate=cost(4, 5),
        name="level_two_rows",
    )(y_32, gain, y_33, near_data, far_data, other_data, out)
    return (out[None, None], data[None, None])


def solution(mesh):
    placed = (P("gz", "box", None, None), P("gz", "box", None, None), P())
    return jax.shard_map(
        local,
        mesh=mesh,
        in_specs=placed,
        out_specs=(P("gz", "box", None, None), P("gz", "box", None, None)),
        check_vma=False,
    )
```

time: 90.3 us -> 105 us (1.16); the launches traced: 88.6 us -> 105 us
  Pallas kernels: 77.3 us -> 97.2 us
  local copies, waits for them, and re-layouts: 4.73 us -> 0.36 us
    pallas_call x1, Pallas kernels: 16.1 us -> 29.8 us  [local(): pl.pallas_call(top_kernel, out_shape=[jax.ShapeDtypeStruct((face, points)...]
    pallas_call x3 -> x1, Pallas kernels: 43.5 us -> 52.7 us  [local(): pl.pallas_call(sums_kernel, out_shape=[square, square, rows, rows], in_sp...]
    unnamed x12 -> x8, local copies, waits for them, and re-layouts: 4.38 us -> 0.02 us
    pallas_call x1, Pallas kernels: 14.7 us -> 11.9 us  [local(): pl.pallas_call(near_kernel, out_shape=[square] * 5, in_specs=[ANY], out_s...]
  transfers between devices with their start and end apart: 4 -> 4, of which waited for: 0 -> 0; matrix products, arithmetic and copies ran while one was open for 1% -> 1% of each run, Pallas kernels for 84% -> 90%
where the time goes in v3:
time: 105 us
  Pallas kernels  97.2 us (93%)
  starting transfers between devices  5.83 us (6%)
    pallas_call x1, Pallas kernels, local(): pl.pallas_call(sums_kernel, out_shape=[square, square, rows, rows], in_sp...  52.7 us
    pallas_call x1, Pallas kernels, local(): pl.pallas_call(top_kernel, out_shape=[jax.ShapeDtypeStruct((face, points)...  29.8 us
    pallas_call x1, Pallas kernels, local(): pl.pallas_call(near_kernel, out_shape=[square] * 5, in_specs=[ANY], out_s...  11.9 us
    ppermute x4, starting transfers between devices, swapped(): return lax.ppermute(block, axis, route)  5.83 us
    pallas_call x1, Pallas kernels, local(): pl.pallas_call(last_kernel, out_shape=[jax.ShapeDtypeStruct((face, points...  2.81 us
  transfers between devices with their start and end apart: 4, of which 0 were waited for; matrix products, arithmetic and copies ran while one was open for 1% of the time, Pallas kernels for 90%

profile of v3, /device:TPU:8, one launch (start us, length us, event | category | flops | bytes accessed | tf_op | source)
XLA Modules:
  0.0 105.2 jit_solution(11605300299161155125)
XLA Ops:
  0.6 0.0 copy-start.3
  0.6 0.1 collective-permute-start.2
  0.7 11.9 %level_one_near.1 = (f32[512,512]{1,0:T(8,128)}, f32[512,512]{1,0:T(8,128)}, f32[512,512]{1,0:T(8,128)}, f32[512,512]{1,0:T(8,128)}, f32[512,512]{1,0:T(8,128)}) custom-call(f32[1,2,1024,1024]{3,2,1,0:T(8,128)} %maps.3), custom_call_target="tpu_custom_call" | custom-call | flops 7247757312 | bytes 11534336 | tf_op jit(solution)/shard_map/level_one_near/pallas_call | solution.py:566
  12.6 2.3 %collective-permute-start.1 = (f32[512,512]{1,0:T(8,128)}, f32[512,512]{1,0:T(8,128)S(1)}, u32[]{:S(2)}, u32[]{:S(2)}) collective-permute-start(f32[512,512]{1,0:T(8,128)} %get-tuple-element.16.o_33_in), channel_id=1, source_target_pairs={{0,1},{1,0},{2,3},{3,2},{4,5},{5,4},{6,7},{7,6},{8,9},{9,8},{10,11... | collective-permute-start | bytes 3145736 | tf_op jit(solution)/shard_map/ppermute | solution.py:24
  14.9 0.1 collective-permute-start
  15.0 0.0 copy-done.3
  15.0 0.1 reshape.18
  15.1 0.2 dynamic-slice_reduce_fusion
  15.3 0.1 pad_add_fusion
  15.4 0.1 broadcast_multiply_fusion
  15.5 0.1 mul.42
  15.5 0.6 add_multiply_fusion.cas
  16.2 0.0 collective-permute-done.2
  16.2 0.0 copy-start.2
  16.2 52.7 %hartley_sums.1 = (f32[512,512]{1,0:T(8,128)}, f32[512,512]{1,0:T(8,128)}, f32[16,512]{1,0:T(8,128)}, f32[16,512]{1,0:T(8,128)}) custom-call(f32[512]{0:T(512)} %add_multiply_fusion.cas, f32[16,32,1024]{2,1,0:T(8,128)} %bitcast.5, f32[16,32,1024]{2,1,0:T(8,128)} %bitcast.1.other_in, f32[1,2,1024,1024]{3,2,1,0:T(8,128)} %maps.3, ...), custom_call_target="tpu_custom_call" | custom-call | flops 26843545600 | bytes 5242880 | tf_op jit(solution)/shard_map/hartley_sums/pallas_call | solution.py:586
  68.9 3.3 %collective-permute-start.3 = (f32[16,512]{1,0:T(8,128)}, f32[16,512]{1,0:T(8,128)S(1)}, u32[]{:S(2)}, u32[]{:S(2)}) collective-permute-start(f32[16,512]{1,0:T(8,128)} %get-tuple-element.23.near_data), channel_id=1, source_target_pairs={{0,1},{1,0},{2,3},{3,2},{4,5},{5,4},{6,7},{7,6},{8,9},{9,8},{10,11... | collective-permute-start | bytes 98312 | tf_op jit(solution)/shard_map/ppermute | solution.py:24
  72.3 0.0 collective-permute-done.1.y_33_in.y_33
  72.3 0.0 copy-done.2
  72.3 0.0 copy-start
  72.3 0.0 copy-start.1
  72.3 29.8 %level_two_gain.1 = (f32[512,1024]{1,0:T(8,128)}, f32[512,512]{1,0:T(8,128)S(1)}) custom-call(f32[512,512]{1,0:T(8,128)S(1)} %collective-permute-done.1.y_33_in.y_33, f32[512,512]{1,0:T(8,128)S(1)} %copy-done.2, f32[512,512]{1,0:T(8,128)} %get-tuple-element.15.o_31_in, f32[512,512]{1,0:T(8,128)} %get-tuple-element.20.o_13_in, ...), custom_call_target="tpu_custom_call" | custom-call | flops 5905580032 | bytes 8388608 | tf_op jit(solution)/shard_map/level_two_gain/pallas_call | solution.py:619
  102.1 0.0 collective-permute-done.y_32
  102.1 0.0 collective-permute-done.3.other_data
  102.1 0.0 copy-done
  102.1 0.0 copy-done.1
  102.1 2.8 %level_two_rows.1 = (f32[512,1024]{1,0:T(8,128)}, f32[16,512]{1,0:T(8,128)}) custom-call(f32[512,512]{1,0:T(8,128)S(1)} %collective-permute-done.y_32, f32[512,512]{1,0:T(8,128)S(1)} %get-tuple-element.22.gain, f32[512,512]{1,0:T(8,128)S(1)} %collective-permute-done.1.y_33_in.y_33, f32[16,512]{1,0:T(8,128)S(1)} %copy-done, ...), custom_call_target="tpu_custom_call", output_to_operand_aliasing={{0}: (6, {})} | custom-call | flops 1073741824 | bytes 5242880 | tf_op jit(solution)/shard_map/level_two_rows/pallas_call | solution.py:630
  (1 shorter events, 0.0 us)
Async XLA Ops:
  0.6 14.4 %copy-start.3 = (s32[32]{0:T(128)S(1)}, s32[32]{0:T(128)}, u32[]{:S(2)}) copy-start(s32[32]{0:T(128)} %param.5) | copy-start | bytes 388
  0.6 15.5 %collective-permute-start.2 = (f32[16,2,16,1024]{3,2,1,0:T(8,128)}, f32[16,2,16,1024]{3,2,1,0:T(8,128)}, u32[]{:S(2)}, u32[]{:S(2)}) collective-permute-start(f32[16,2,16,1024]{3,2,1,0:T(8,128)} %param.3), channel_id=1, source_target_pairs={{0,8},{8,0},{16,24},{24,16},{32,40},{40,32},{48,56},{56,48},{64,72... | collective-permute-start | bytes 6291464 | tf_op jit(solution)/shard_map/ppermute | solution.py:24
  12.6 59.6 %collective-permute-start.1 = (f32[512,512]{1,0:T(8,128)}, f32[512,512]{1,0:T(8,128)S(1)}, u32[]{:S(2)}, u32[]{:S(2)}) collective-permute-start(f32[512,512]{1,0:T(8,128)} %get-tuple-element.16.o_33_in), channel_id=1, source_target_pairs={{0,1},{1,0},{2,3},{3,2},{4,5},{5,4},{6,7},{7,6},{8,9},{9,8},{10,11... | collective-permute-start | bytes 3145736 | tf_op jit(solution)/shard_map/ppermute | solution.py:24
  14.9 87.2 %collective-permute-start = (f32[512,512]{1,0:T(8,128)}, f32[512,512]{1,0:T(8,128)S(1)}, u32[]{:S(2)}, u32[]{:S(2)}) collective-permute-start(f32[512,512]{1,0:T(8,128)} %get-tuple-element.15.o_31_in), channel_id=1, source_target_pairs={{0,1},{1,0},{2,3},{3,2},{4,5},{5,4},{6,7},{7,6},{8,9},{9,8},{10,11... | collective-permute-start | bytes 3145736 | tf_op jit(solution)/shard_map/ppermute | solution.py:24
  16.2 56.1 %copy-start.2 = (f32[512,512]{1,0:T(8,128)S(1)}, f32[512,512]{1,0:T(8,128)}, u32[]{:S(2)}) copy-start(f32[512,512]{1,0:T(8,128)} %get-tuple-element.16.o_33_in) | copy-start | bytes 3145732
  68.9 33.2 %collective-permute-start.3 = (f32[16,512]{1,0:T(8,128)}, f32[16,512]{1,0:T(8,128)S(1)}, u32[]{:S(2)}, u32[]{:S(2)}) collective-permute-start(f32[16,512]{1,0:T(8,128)} %get-tuple-element.23.near_data), channel_id=1, source_target_pairs={{0,1},{1,0},{2,3},{3,2},{4,5},{5,4},{6,7},{7,6},{8,9},{9,8},{10,11... | collective-permute-start | bytes 98312 | tf_op jit(solution)/shard_map/ppermute | solution.py:24
  72.3 29.9 %copy-start = (f32[16,512]{1,0:T(8,128)S(1)}, f32[16,512]{1,0:T(8,128)}, u32[]{:S(2)}) copy-start(f32[16,512]{1,0:T(8,128)} %get-tuple-element.23.near_data) | copy-start | bytes 98308
  72.3 29.9 %copy-start.1 = (f32[16,512]{1,0:T(8,128)S(1)}, f32[16,512]{1,0:T(8,128)}, u32[]{:S(2)}) copy-start(f32[16,512]{1,0:T(8,128)} %get-tuple-element.24.far_data) | copy-start | bytes 98308

commit v4 on v3

v4 whole, which is shorter than its diff:
```python
import jax
import jax.numpy as jnp
from jax import lax
from jax.experimental import pallas as pl
from jax.experimental.pallas import tpu as pltpu
from jax.sharding import PartitionSpec as P

NZ = 512
MESH = pl.DeviceIdType.MESH
F32 = jnp.float32
BF16 = jnp.bfloat16
HALF = 256
FINE = 3.6e-9
VMEM_LIMIT = 60 * 1024 * 1024
JOINT_VMEM = 60 * 1024 * 1024
LAST_VMEM = 60 * 1024 * 1024


def split(value):
    high = value.astype(BF16)
    return high, (value - high.astype(F32)).astype(BF16)


def put_left(ref, start, value):
    face = value.shape[1]
    high, low = split(value)
    rows = pl.ds(start, value.shape[0])
    ref[rows, 0:face] = high
    ref[rows, face : 2 * face] = high
    ref[rows, 2 * face : 3 * face] = low


def put_right(ref, start, value):
    face = ref.shape[0] // 3
    high, low = split(value)
    count = value.shape[0]
    ref[pl.ds(start, count), :] = high
    ref[pl.ds(face + start, count), :] = low
    ref[pl.ds(2 * face + start, count), :] = high


def fill(put, ref, source):
    for start in range(0, source.shape[0], HALF):
        put(ref, start, source[start : start + HALF, :])


def product(left, right, start):
    return jnp.dot(left[start : start + HALF, :], right[...], preferred_element_type=F32)


def halves(face):
    return range(0, face, HALF)


def eye_rows(start, face):
    row = lax.broadcasted_iota(jnp.int32, (HALF, face), 0) + start
    col = lax.broadcasted_iota(jnp.int32, (HALF, face), 1)
    return jnp.where(row == col, 1.0, 0.0).astype(F32)


def chunk_sum(part):
    return jnp.sum(part.reshape(-1, 8, part.shape[1]), axis=0)


def invert(k_left, total, power, rough, spare):
    face = total.shape[0]

    def raise_power():
        parts = [
            jnp.dot(power[s : s + HALF, :], power[...], preferred_element_type=F32)
            for s in halves(face)
        ]
        for s, part in zip(halves(face), parts):
            power[s : s + HALF, :] = part.astype(BF16)

    def gather():
        for s in halves(face):
            rough[s : s + HALF, :] = total[s : s + HALF, :].astype(BF16)
        for s in halves(face):
            total[s : s + HALF, :] += jnp.dot(
                rough[s : s + HALF, :], power[...], preferred_element_type=F32
            )

    raise_power()
    for _ in range(3):
        gather()
        raise_power()
    gather()
    for s in halves(face):
        rough[s : s + HALF, :] = total[s : s + HALF, :].astype(BF16)
    first = jnp.zeros((8, face), F32)
    for s in halves(face):
        part = jnp.dot(
            k_left[s : s + HALF, 0:face], rough[...], preferred_element_type=F32
        ) + jnp.dot(
            k_left[s : s + HALF, 2 * face : 3 * face], rough[...], preferred_element_type=F32
        )
        part = part - rough[s : s + HALF, :].astype(F32) + eye_rows(s, face)
        spare[s : s + HALF, :] = part
        power[s : s + HALF, :] = part.astype(BF16)
        first += chunk_sum(part * part)
    second = jnp.zeros((8, face), F32)
    for s in halves(face):
        part = jnp.dot(power[s : s + HALF, :], power[...], preferred_element_type=F32)
        second += chunk_sum(part * part)
        spare[s : s + HALF, :] += part
    for s in halves(face):
        power[s : s + HALF, :] = spare[s : s + HALF, :].astype(BF16)
    for s in halves(face):
        total[s : s + HALF, :] = rough[s : s + HALF, :].astype(F32) + jnp.dot(
            rough[s : s + HALF, :], power[...], preferred_element_type=F32
        )
    return first, second


def poor(first, second):
    first, second = jnp.sum(first), jnp.sum(second)
    return jnp.logical_not((first < 0.25) & (first * second < FINE))


def careful(k_left, total, left, right, spare):
    face = total.shape[0]
    for s in halves(face):
        kept = k_left[s : s + HALF, 0:face].astype(F32)
        kept += k_left[s : s + HALF, 2 * face : 3 * face].astype(F32)
        spare[s : s + HALF, :] = kept
        total[s : s + HALF, :] = kept + eye_rows(s, face)

    def raise_power():
        fill(put_left, left, spare)
        fill(put_right, right, spare)
        size = 0.0
        for s in halves(face):
            part = product(left, right, s)
            spare[s : s + HALF, :] = part
            size += jnp.sum(part * part)
        return size

    def squaring(state):
        count, _ = state
        fill(put_left, left, total)
        fill(put_right, right, spare)
        for s in halves(face):
            total[s : s + HALF, :] += product(left, right, s)
        return count + 1, raise_power()

    lax.while_loop(
        lambda state: (state[1] > 1e-15) & (state[0] < 48),
        squaring,
        (jnp.int32(0), raise_power()),
    )

    def newton(state):
        count, last, _ = state
        fill(put_right, right, total)
        size = 0.0
        for s in halves(face):
            part = product(k_left, right, s) - total[s : s + HALF, :] + eye_rows(s, face)
            spare[s : s + HALF, :] = part
            size += jnp.sum(part * part)
        better = size < 0.25 * last

        @pl.when(better)
        def _():
            fill(put_left, left, total)
            fill(put_right, right, spare)
            for s in halves(face):
                total[s : s + HALF, :] += product(left, right, s)

        return count + 1, size, better

    lax.while_loop(
        lambda state: state[2] & (state[0] < 4),
        newton,
        (jnp.int32(0), jnp.float32(1.0), jnp.bool_(True)),
    )


def fetcher(maps, sems, face):
    def fetch(slot, leaf, row, col, dst):
        copy = pltpu.make_async_copy(
            maps.at[
                0,
                leaf,
                pl.ds(pl.multiple_of(row * face, face), face),
                pl.ds(pl.multiple_of(col * face, face), face),
            ],
            dst,
            sems.at[slot],
        )
        copy.start()
        return copy

    return fetch


def started(src, dst, sem):
    copy = pltpu.make_async_copy(src, dst, sem)
    copy.start()
    return copy


def cas_rows(mode_ids, planes, shape):
    here = lax.axis_index("gz")
    core = here % 2
    row = lax.broadcasted_iota(jnp.int32, shape, 0)
    col = lax.broadcasted_iota(jnp.int32, shape, 1)
    mode = jnp.zeros(shape, jnp.int32)
    for slot in range(shape[0]):
        mode = jnp.where(row == slot, mode_ids[2 * slot + core], mode)
    start = jnp.where(col < planes, here * planes, (here - 2 * core) * planes)
    phase = mode * (start + col) & (NZ - 1)
    angle = phase.astype(F32) * (2.0 * jnp.pi / NZ)
    return (jnp.cos(angle) + jnp.sin(angle)) / NZ**0.5


def near_kernel(mode_ids, maps, cas, o_33_out, gain_out, inv_out, through_out, *scratch):
    a_33, b_33, b_32, b_23, b_22, gain, inv, through = scratch[:8]
    l_one, l_two, k_left, r_one, r_two, power, rough, spare, sems = scratch[8:]
    face = a_33.shape[0]
    far = lax.axis_index("box") % 2
    near = 1 - far
    fetch = fetcher(maps, sems, face)
    copies = [
        fetch(0, far, near, near, a_33),
        fetch(1, near, far, far, b_33),
        fetch(2, near, far, near, b_32),
        fetch(3, near, near, far, b_23),
        fetch(4, near, near, near, b_22),
    ]
    cas[...] = cas_rows(mode_ids, NZ // lax.axis_size("gz"), cas.shape)
    copies[0].wait()
    fill(put_left, l_one, a_33)
    copies[1].wait()
    fill(put_right, r_one, b_33)
    for s in halves(face):
        part = product(l_one, r_one, s)
        put_left(k_left, s, part)
        power[s : s + HALF, :] = part.astype(BF16)
        inv[s : s + HALF, :] = part + eye_rows(s, face)
    copies[2].wait()
    fill(put_right, r_one, b_32)
    for s in halves(face):
        part = product(l_one, r_one, s)
        through[s : s + HALF, :] = part
        put_right(r_two, s, part)
    outs = [started(through, through_out, sems.at[5])]
    first, second = invert(k_left, inv, power, rough, spare)

    @pl.when(poor(first, second))
    def _():
        careful(k_left, inv, l_one, r_one, spare)

    outs.append(started(inv, inv_out, sems.at[6]))
    copies[3].wait()
    fill(put_left, l_one, b_23)
    fill(put_right, r_one, inv)
    for s in halves(face):
        part = product(l_one, r_one, s)
        gain[s : s + HALF, :] = part
        put_left(l_two, s, part)
    outs.append(started(gain, gain_out, sems.at[7]))
    copies[4].wait()
    for s in halves(face):
        b_22[s : s + HALF, :] += product(l_two, r_two, s)
    outs.append(started(b_22, o_33_out, sems.at[8]))
    for copy in outs:
        copy.wait()


def keep_pair(highs, lows, start, value):
    high, low = split(value)
    highs[start : start + value.shape[0], :] = high
    lows[start : start + value.shape[0], :] = low


def rows_times(rows, highs, lows):
    r_high, r_low = split(rows)

    def dot(left, right):
        return lax.dot_general(
            left, right, (((1,), (1,)), ((), ())), preferred_element_type=F32
        )

    return dot(r_high, highs[...]) + (dot(r_low, highs[...]) + dot(r_high, lows[...]))


def last_kernel(norms, data_in, *refs):
    y_32_in, gain_in, own_in, *rest, out, data = refs[:13]
    y_32, gain, own, y_33, o_33, o_31, o_13, o_11, near_data, far_data, beyond = refs[13:24]
    k_left, left, right, inv, other, sems = refs[24:]
    face = gain.shape[0]
    far = lax.axis_index("box") % 2
    scale = (2.0 * face) ** 0.5
    copies = [
        started(src, dst, sems.at[slot])
        for slot, (src, dst) in enumerate(((gain_in, gain), (y_32_in, y_32)))
    ]
    data[...] = data_in[...]
    bad = poor(norms[0:8, :], norms[8:16, :])
    own_cols = pl.ds(pl.multiple_of(far * face, face), face)

    @pl.when(jnp.logical_not(bad))
    def _():
        started(own_in, out.at[:, own_cols], sems.at[8])

    for copy in copies:
        copy.wait()

    @pl.when(bad)
    def _():
        held = (y_33, o_33, o_31, o_13, o_11, near_data, far_data, beyond)
        for slot, (src, dst) in enumerate(zip(rest, held)):
            started(src, dst, sems.at[slot]).wait()
        fill(put_left, left, y_33)
        fill(put_right, right, o_33)
        for s in halves(face):
            put_left(k_left, s, product(left, right, s))
        careful(k_left, inv, left, right, other)
        fill(put_left, left, o_13)
        fill(put_right, right, inv)
        for s in halves(face):
            gain[s : s + HALF, :] = product(left, right, s)
        fill(put_left, left, y_33)
        fill(put_right, right, o_31)
        for s in halves(face):
            other[s : s + HALF, :] = product(left, right, s)
        fill(put_left, left, gain)
        fill(put_right, right, other)
        for s in halves(face):
            own[s : s + HALF, :] = (o_11[s : s + HALF, :] + product(left, right, s)) * scale
        jump = rows_times(near_data[...], *split(y_33[...])) - beyond[...]
        data[...] = far_data[...] + rows_times(jump, *split(gain[...]))
        started(own, out.at[:, own_cols], sems.at[8])

    copies = [pltpu.make_async_copy(own, out.at[:, own_cols], sems.at[8])]
    fill(put_left, left, gain)
    fill(put_right, right, y_32)
    other_cols = pl.ds(pl.multiple_of((1 - far) * face, face), face)
    for s in halves(face):
        rows = slice(s, s + HALF)
        other[rows, :] = product(left, right, s) * -scale
        copies.append(started(other.at[rows, :], out.at[rows, other_cols], sems.at[1 + s // HALF]))
    for copy in copies:
        copy.wait()


def joint_kernel(
    cas, own_in, maps, inv_in, through_in, near_gain_in, o_33_in, *refs
):
    norms, data, y_32, gain_out, own_out, y_33_out, o_31_out, o_13_out, o_11_out = refs[:9]
    near_out, far_out, beyond_out = refs[9:12]
    scratch = refs[12:]
    sent, got, mine, side_sent, side_got, send_sem, recv_sem = scratch[:7]
    near_data, far_data, beyond = scratch[7:10]
    a_13, b_33, b_32, a_11, a_31, a_33, inv, through, near_gain, gain, o_13 = scratch[10:21]
    o_33, o_31, y_33, total, spare = scratch[21:26]
    left, r_one, r_two, l_two, k_left, power, rough = scratch[26:33]
    near_high, near_low, far_high, far_low, own, other, sems = scratch[33:]
    face = inv.shape[0]
    far = lax.axis_index("box") % 2
    near = 1 - far
    fetch = fetcher(maps, sems, face)
    planes_in = started(own_in, own, sems.at[11])
    in_33 = started(o_33_in, o_33, sems.at[13])
    gain_in = started(near_gain_in, near_gain, sems.at[8])
    in_31 = fetch(4, far, near, far, a_31)
    copies_in = [
        fetch(0, far, far, near, a_13),
        fetch(1, near, far, far, b_33),
        fetch(2, near, far, near, b_32),
        started(inv_in, inv, sems.at[3]),
        fetch(5, far, far, far, a_11),
        started(through_in, through, sems.at[6]),
        fetch(7, far, near, near, a_33),
    ]
    here = lax.axis_index("gz")
    core, z, x = here % 2, here // 2 % 8, here // 16

    def device(x_at, z_at, core_at=core):
        return {"gz": x_at * 16 + z_at * 2 + core_at}

    ring = (device(x, (z + 1) % 8), device(x, (z + 7) % 8))
    beside = device(1 - x, z)
    place = lax.axis_index("box")
    planes = own.shape[0]
    partner = {"box": place + 1 - 2 * far}
    barrier = pltpu.get_barrier_semaphore()
    sibling = device(x, z, 1 - core)
    for target in (partner, sibling, *ring, beside):
        pl.semaphore_signal(barrier, inc=1, device_id=target, device_id_type=MESH)

    def post(src, dst, slot, target):
        return pltpu.make_async_remote_copy(
            src_ref=src,
            dst_ref=dst,
            send_sem=send_sem.at[2, slot],
            recv_sem=recv_sem.at[2, slot],
            device_id=target,
            device_id_type=MESH,
        )

    side = post(side_sent, side_got, 0, beside)
    first_block = post(o_33_in, y_33, 1, partner)
    second_block = post(o_31, y_32, 2, partner)
    news = post(near_data, beyond, 3, partner)
    swap = post(own_in, other, 4, sibling)
    pl.semaphore_wait(barrier, 5)
    first_block.start()
    swap.start()

    def term(x_to, z_to, store):
        row = x_to * 8 + z_to

        def block(part, carry):
            rows = pl.ds(pl.multiple_of(part * 8, 8), 8)
            total = cas[row, 0] * own[0, rows, :]
            for k in range(1, planes):
                total += cas[row, k] * own[k, rows, :]
            for k in range(planes):
                total += cas[row, planes + k] * other[k, rows, :]
            store(rows, total)
            return carry

        lax.fori_loop(0, own.shape[1] // 8, block, 0)

    def message(way, index):
        return pltpu.make_async_remote_copy(
            src_ref=sent.at[way, index],
            dst_ref=got.at[way, index],
            send_sem=send_sem.at[way, index],
            recv_sem=recv_sem.at[way, index],
            device_id=ring[way],
            device_id_type=MESH,
        )

    copies_out = []

    def send_second():
        gain_in.wait()
        in_31.wait()
        fill(put_left, left, near_gain)
        fill(put_right, r_one, a_31)
        for s in halves(face):
            o_31[s : s + HALF, :] = -product(left, r_one, s)
        second_block.start()
        copies_out.append(started(o_31, o_31_out, sems.at[8]))

    def work_0():
        copies_in[0].wait()
        fill(put_left, left, a_13)
        copies_in[1].wait()
        fill(put_right, r_two, b_33)
        for s in halves(face):
            gain[s : s + HALF, :] = product(left, r_two, s)

    def work_1():
        copies_in[2].wait()
        fill(put_right, r_two, b_32)
        for s in halves(face):
            o_13[s : s + HALF, :] = -product(left, r_two, s)

    def work_2():
        copies_in[3].wait()
        fill(put_left, left, gain)
        fill(put_right, r_two, inv)
        for s in halves(face):
            gain[s : s + HALF, :] = product(left, r_two, s)

    def work_3():
        fill(put_left, left, gain)
        copies_in[4].wait()
        for s in halves(face):
            a_11[s : s + HALF, :] += product(left, r_one, s)
        copies_out.append(started(a_11, o_11_out, sems.at[9]))

    def work_4():
        copies_in[5].wait()
        fill(put_right, r_two, through)
        for s in halves(face):
            o_13[s : s + HALF, :] -= product(left, r_two, s)
        copies_out.append(started(o_13, o_13_out, sems.at[10]))

    def work_5():
        copies_in[6].wait()
        for s in halves(face):
            rows = slice(s, s + HALF)
            keep_pair(far_high, far_low, s, a_33[rows, :])
            keep_pair(far_high, far_low, face + s, a_13[rows, :])
            keep_pair(near_high, near_low, s, near_gain[rows, :])
            keep_pair(near_high, near_low, face + s, gain[rows, :])

    send_second()
    work_0()
    planes_in.wait()
    swap.wait_recv()
    work = (work_1, work_2, work_3, work_4, work_5)
    copies = [[message(way, index) for index in range(7)] for way in range(2)]
    for index in range(7):
        step = (index + 3) // 2
        first = index % 2 == 0
        for way in range(2):
            x_to = way if first else 1 - way
            z_to = (z + (5 - step)) % 8 if way == 0 else (z + 8 - (5 - step)) % 8

            def store(rows, total, way=way, index=index):
                sent[way, index, rows, :] = total

            term(x_to, z_to, store)
            if index >= 2:
                copies[way][index - 2].wait_recv()
                sent[way, index] += got[way, index - 2]
            copies[way][index].start()
        if index < len(work):
            work[index]()
    for x_to in range(2):

        def store(rows, total, x_to=x_to):
            mine[x_to, rows, :] = total

        term(x_to, z, store)
    for index in (5, 6):
        for way in range(2):
            copies[way][index].wait_recv()
    away = 1 - x
    side_sent[...] = mine[away] + (got[0, 6 - away] + got[1, 5 + away])
    side.start()
    mine[x] += got[0, 6 - x] + got[1, 5 + x]
    first_block.wait_recv()
    copies_out.append(started(y_33, y_33_out, sems.at[0]))
    in_33.wait()
    fill(put_left, l_two, y_33)
    fill(put_right, r_one, o_33)
    for s in halves(face):
        part = product(l_two, r_one, s)
        put_left(k_left, s, part)
        power[s : s + HALF, :] = part.astype(BF16)
        total[s : s + HALF, :] = part + eye_rows(s, face)
    side.wait_recv()
    mine[x] += side_got[...]
    rhs = near_data.shape[0]

    def info(leaf, side):
        return mine[
            x,
            pl.ds(pl.multiple_of(leaf * rhs, rhs), rhs),
            pl.ds(pl.multiple_of(side * face, face), face),
        ]

    known = rows_times(info(near, far), far_high, far_low)
    jump = info(far, near) - known[:, 0:face]
    moved = rows_times(jump, near_high, near_low)
    near_data[...] = info(near, near) - moved[:, 0:face]
    news.start()
    far_data[...] = info(far, far) + moved[:, face : 2 * face] - known[:, face : 2 * face]
    copies_out.append(started(near_data, near_out, sems.at[1]))
    copies_out.append(started(far_data, far_out, sems.at[2]))
    fill(put_right, r_one, o_31)
    for s in halves(face):
        put_right(r_two, s, product(l_two, r_one, s))
    norms[0:8, :], norms[8:16, :] = invert(k_left, total, power, rough, spare)
    fill(put_left, left, o_13)
    fill(put_right, r_one, total)
    for s in halves(face):
        part = product(left, r_one, s)
        gain[s : s + HALF, :] = part
        put_left(k_left, s, part)
    copies_out.append(started(gain, gain_out, sems.at[4]))
    scale = (2.0 * face) ** 0.5
    for s in halves(face):
        total[s : s + HALF, :] = (a_11[s : s + HALF, :] + product(k_left, r_two, s)) * scale
    copies_out.append(started(total, own_out, sems.at[5]))
    news.wait_recv()
    copies_out.append(started(beyond, beyond_out, sems.at[3]))
    jump = rows_times(near_data[...], l_two.at[:, 0:face], l_two.at[:, 2 * face :])
    jump -= beyond[...]
    data[...] = far_data[...] + rows_times(
        jump, k_left.at[:, 0:face], k_left.at[:, 2 * face :]
    )
    for way in range(2):
        for index in range(7):
            copies[way][index].wait_send()
    for copy in (side, first_block, second_block, news, swap):
        copy.wait_send()
    for copy in copies_out:
        copy.wait()
    second_block.wait_recv()


def vmem_specs(count):
    return [pl.BlockSpec(memory_space=pltpu.VMEM)] * count


ANY = pl.BlockSpec(memory_space=pl.ANY)


def local(sources, leaf_maps, mode_ids):
    planes, boxes, rhs, points = sources.shape
    face = points // 2
    square = jax.ShapeDtypeStruct((face, face), F32)
    rows = jax.ShapeDtypeStruct((rhs, face), F32)
    full = pltpu.VMEM((face, face), F32)
    short = pltpu.VMEM((face, face), BF16)
    left = pltpu.VMEM((face, 3 * face), BF16)
    right = pltpu.VMEM((3 * face, face), BF16)
    params = pltpu.CompilerParams(vmem_limit_bytes=VMEM_LIMIT)

    def cost(units, size):
        return pl.CostEstimate(
            flops=units * 2 * face**3, bytes_accessed=size * 4 * face**2, transcendentals=0
        )

    cas, o_33, near_gain, inv, through = pl.pallas_call(
        near_kernel,
        out_shape=[jax.ShapeDtypeStruct((mode_ids.shape[0] // 2, 128), F32)] + [square] * 4,
        in_specs=[pl.BlockSpec(memory_space=pltpu.SMEM), ANY],
        out_specs=vmem_specs(1) + [ANY] * 4,
        scratch_shapes=[full] * 8
        + [left, left, left, right, right, short, short, full, pltpu.SemaphoreType.DMA((9,))],
        compiler_params=params,
        cost_estimate=cost(24, 9),
        name="level_one_near",
    )(mode_ids, leaf_maps)
    line = (boxes * rhs, points)
    pair = pltpu.VMEM((2 * face, face), BF16)
    narrow = pltpu.VMEM((rhs, face), F32)
    whole = jax.ShapeDtypeStruct((face, points), F32)
    norms, data, *made = pl.pallas_call(
        joint_kernel,
        out_shape=[jax.ShapeDtypeStruct((16, face), F32), rows] + [square] * 7 + [rows] * 3,
        in_specs=[pl.BlockSpec(memory_space=pltpu.SMEM)] + [ANY] * 6,
        out_specs=vmem_specs(2) + [ANY] * 10,
        scratch_shapes=[
            pltpu.VMEM((2, 7, *line), F32),
            pltpu.VMEM((2, 7, *line), F32),
            pltpu.VMEM((2, *line), F32),
            pltpu.VMEM(line, F32),
            pltpu.VMEM(line, F32),
            pltpu.SemaphoreType.DMA((3, 7)),
            pltpu.SemaphoreType.DMA((3, 7)),
            narrow,
            narrow,
            narrow,
        ]
        + [full] * 16
        + [left, right, right, left, left, short, short]
        + [pair, pair, pair, pair]
        + [pltpu.VMEM((planes, *line), F32)] * 2
        + [pltpu.SemaphoreType.DMA((16,))],
        compiler_params=pltpu.CompilerParams(
            vmem_limit_bytes=JOINT_VMEM, collective_id=0, has_side_effects=True
        ),
        cost_estimate=cost(100, 20),
        name="exchange_sums_level_two",
    )(
        cas,
        sources.reshape(planes, *line),
        leaf_maps,
        inv,
        through,
        near_gain,
        o_33,
    )
    y_32, gain, own, y_33, o_31, o_13, o_11, near_data, far_data, beyond = made
    out, data = pl.pallas_call(
        last_kernel,
        out_shape=[whole, rows],
        in_specs=vmem_specs(2) + [ANY] * 11,
        out_specs=[ANY] + vmem_specs(1),
        scratch_shapes=[full] * 8
        + [narrow] * 3
        + [left, left, right, full, full, pltpu.SemaphoreType.DMA((9,))],
        compiler_params=pltpu.CompilerParams(vmem_limit_bytes=LAST_VMEM),
        cost_estimate=cost(4, 5),
        name="level_two_rows",
    )(norms, data, y_32, gain, own, y_33, o_33, o_31, o_13, o_11, near_data, far_data, beyond)
    return (out[None, None], data[None, None])


def solution(mesh):
    placed = (P("gz", "box", None, None), P("gz", "box", None, None), P())
    return jax.shard_map(
        local,
        mesh=mesh,
        in_specs=placed,
        out_specs=(P("gz", "box", None, None), P("gz", "box", None, None)),
        check_vma=False,
    )
```

time: 105 us -> 119 us (1.13)
  the two profiles are of different devices: /device:TPU:8 before, /device:TPU:91 now
where the time goes in v4:
time: 119 us
  Pallas kernels  118 us (99%)
    pallas_call x1, Pallas kernels, local(): pl.pallas_call(joint_kernel, out_shape=[jax.ShapeDtypeStruct((16, face),...  71.4 us
    pallas_call x1, Pallas kernels, local(): pl.pallas_call(last_kernel, out_shape=[whole, rows], in_specs=vmem_specs(...  34.5 us
    pallas_call x1, Pallas kernels, local(): pl.pallas_call(near_kernel, out_shape=[jax.ShapeDtypeStruct((mode_ids.sha...  12.1 us

profile of v4, /device:TPU:91, one launch (start us, length us, event | category | flops | bytes accessed | tf_op | source)
XLA Modules:
  0.0 118.8 jit_solution(14911570103371446445)
XLA Ops:
  0.6 12.1 %level_one_near.1 = (f32[16,128]{1,0:T(8,128)}, f32[512,512]{1,0:T(8,128)}, f32[512,512]{1,0:T(8,128)}, f32[512,512]{1,0:T(8,128)}, f32[512,512]{1,0:T(8,128)}) custom-call(s32[32]{0:T(128)} %mode_ids.1, f32[1,2,1024,1024]{3,2,1,0:T(8,128)} %maps.3), custom_call_target="tpu_custom_call" | custom-call | flops 6442450944 | bytes 9437184 | tf_op jit(solution)/shard_map/level_one_near/pallas_call | solution.py:613
  12.7 71.4 %exchange_sums_level_two.1 = (f32[16,512]{1,0:T(8,128)}, f32[16,512]{1,0:T(8,128)}, f32[512,512]{1,0:T(8,128)}, f32[512,512]{1,0:T(8,128)}, f32[512,512]{1,0:T(8...) custom-call(f32[16,128]{1,0:T(8,128)} %get-tuple-element.21.cas, ...), custom_call_target="tpu_custom_call" | custom-call | flops 26843545600 | bytes 20971520 | tf_op jit(solution)/shard_map/exchange_sums_level_two/pallas_call | solution.py:628
  84.2 34.5 %level_two_rows.1 = (f32[512,1024]{1,0:T(8,128)}, f32[16,512]{1,0:T(8,128)}) custom-call(f32[16,512]{1,0:T(8,128)} %get-tuple-element.26.norms, f32[16,512]{1,0:T(8,128)} %get-tuple-element.27.data_in, f32[512,512]{1,0:T(8,128)} %get-tuple-element.28.refs_0_, f32[512,512]{1,0:T(8,128)} %get-tuple-element.29.refs_1_, f32[512,512]{1,0:T(8,128)} %get-tuple-element.30.refs_2_, ...), custom_call_target="tpu_custom_call" | custom-call | flops 1073741824 | bytes 5242880 | tf_op jit(solution)/shard_map/level_two_rows/pallas_call | solution.py:665

commit v5 on v3

--- a/solution.py
+++ b/solution.py
@@ -22,12 +22,6 @@
     for low in range(0, count, 2):
         route += [(low, low + 1), (low + 1, low)]
     return lax.ppermute(block, axis, route)
-
-
-def cas_table(mode_list, z_index, length_z):
-    phase = mode_list[:, None] * z_index[None, :] % length_z
-    angle = phase.astype(F32) * (2.0 * jnp.pi / length_z)
-    return (jnp.cos(angle) + jnp.sin(angle)) / jnp.sqrt(jnp.float32(length_z))
 
 
 def split(value):
@@ -213,7 +207,32 @@
     return copy
 
 
-def near_kernel(maps, o_33_out, o_31_out, gain_out, inv_out, through_out, *scratch):
+def cas_rows(mode_ids, planes, shape):
+    here = lax.axis_index("gz")
+    core = here % 2
+    row = lax.broadcasted_iota(jnp.int32, shape, 0)
+    col = lax.broadcasted_iota(jnp.int32, shape, 1)
+    mode = jnp.zeros(shape, jnp.int32)
+    for slot in range(shape[0]):
+        mode = jnp.where(row == slot, mode_ids[2 * slot + core], mode)
+    start = jnp.where(col < planes, here * planes, (here - 2 * core) * planes)
+    phase = mode * (start + col) & (NZ - 1)
+    quarter = (phase + NZ // 8) // (NZ // 4)
+    angle = (phase - quarter * (NZ // 4)).astype(F32) * (2.0 * jnp.pi / NZ)
+    power = angle * angle
+    cosine = jnp.ones(shape, F32)
+    sine = jnp.ones(shape, F32)
+    for k in (5, 4, 3, 2, 1):
+        cosine = 1.0 - power * cosine * (1.0 / ((2 * k - 1) * (2 * k)))
+        sine = 1.0 - power * sine * (1.0 / ((2 * k) * (2 * k + 1)))
+    sine = sine * angle
+    value = jnp.where(quarter % 2 == 0, cosine + sine, cosine - sine)
+    return jnp.where(quarter % 4 < 2, value, -value) * (1.0 / NZ**0.5)
+
+
+def near_kernel(
+    mode_ids, maps, cas, o_33_out, o_31_out, gain_out, inv_out, through_out, *scratch
+):
     a_33, b_33, b_32, b_23, b_22, a_31, gain, inv, through = scratch[:9]
     l_one, l_two, k_left, r_one, r_two, power, rough, spare, sems = scratch[9:]
     face = a_33.shape[0]
@@ -223,14 +242,17 @@
     copies = [
         fetch(0, far, near, near, a_33),
         fetch(1, near, far, far, b_33),
+    ]
+    cas[...] = cas_rows(mode_ids, NZ // lax.axis_size("gz"), cas.shape)
+    copies[0].wait()
+    fill(put_left, l_one, a_33)
+    copies[1].wait()
+    copies += [
         fetch(2, near, far, near, b_32),
         fetch(3, near, near, far, b_23),
         fetch(4, near, near, near, b_22),
         fetch(5, far, near, far, a_31),
     ]
-    copies[0].wait()
-    fill(put_left, l_one, a_33)
-    copies[1].wait()
     fill(put_right, r_one, b_33)
     for s in halves(face):
         part = product(l_one, r_one, s)
@@ -284,38 +306,28 @@
     return dot(r_high, highs[...]) + (dot(r_low, highs[...]) + dot(r_high, lows[...]))
 
 
-def top_kernel(y_33_in, o_33_in, o_31_in, o_13_in, o_11_in, out, gain_out, *scratch):
-    y_33, o_33, o_31, o_13, o_11, gain, inv = scratch[:7]
-    l_one, k_left, r_one, r_two, power, rough, spare, sems = scratch[7:]
+def top_kernel(y_33, o_33, o_31_in, o_13_in, o_11_in, out, gain_out, *scratch):
+    o_31, o_13, o_11, gain, inv = scratch[:5]
+    l_one, k_left, r_one, r_two, power, rough, spare, sems = scratch[5:]
     face = y_33.shape[0]
     far = lax.axis_index("box") % 2
     copies = [
         started(src, dst, sems.at[slot])
-        for slot, (src, dst) in enumerate(
-            (
-                (y_33_in, y_33),
-                (o_33_in, o_33),
-                (o_31_in, o_31),
-                (o_13_in, o_13),
-                (o_11_in, o_11),
-            )
-        )
+        for slot, (src, dst) in enumerate(((o_31_in, o_31), (o_13_in, o_13), (o_11_in, o_11)))
     ]
-    copies[0].wait()
     fill(put_left, l_one, y_33)
-    copies[1].wait()
     fill(put_right, r_one, o_33)
     for s in halves(face):
         part = product(l_one, r_one, s)
         put_left(k_left, s, part)
         power[s : s + HALF, :] = part.astype(BF16)
         inv[s : s + HALF, :] = part + eye_rows(s, face)
-    copies[2].wait()
+    copies[0].wait()
     fill(put_right, r_one, o_31)
     for s in halves(face):
         put_right(r_two, s, product(l_one, r_one, s))
     invert(k_left, inv, power, rough, l_one, r_one, spare)
-    copies[3].wait()
+    copies[1].wait()
     fill(put_left, l_one, o_13)
     fill(put_right, r_one, inv)
     for s in halves(face):
@@ -324,7 +336,7 @@
         put_left(k_left, s, part)
     last = [started(gain, gain_out, sems.at[5])]
     scale = (2.0 * face) ** 0.5
-    copies[4].wait()
+    copies[2].wait()
     for s in halves(face):
         o_11[s : s + HALF, :] = (o_11[s : s + HALF, :] + product(k_left, r_two, s)) * scale
         last.append(
@@ -373,6 +385,19 @@
     near = 1 - far
     fetch = fetcher(maps, sems, face)
     planes_in = (started(own_in, own, sems.at[11]), started(other_in, other, sems.at[12]))
+    here = lax.axis_index("gz")
+    core, z, x = here % 2, here // 2 % 8, here // 16
+
+    def device(x_at, z_at):
+        return {"gz": x_at * 16 + z_at * 2 + core}
+
+    ring = (device(x, (z + 1) % 8), device(x, (z + 7) % 8))
+    beside = device(1 - x, z)
+    barrier = pltpu.get_barrier_semaphore()
+    for target in (*ring, beside):
+        pl.semaphore_signal(barrier, inc=1, device_id=target, device_id_type=MESH)
+    for copy in planes_in:
+        copy.wait()
     copies_in = [
         fetch(0, far, far, near, a_13),
         fetch(1, near, far, far, b_33),
@@ -385,30 +410,17 @@
         started(near_gain_in, near_gain, sems.at[8]),
     ]
     planes = own.shape[0]
-    here = lax.axis_index("gz")
-    core, z, x = here % 2, here // 2 % 8, here // 16
-
-    def device(x_at, z_at):
-        return {"gz": x_at * 16 + z_at * 2 + core}
-
-    ring = (device(x, (z + 1) % 8), device(x, (z + 7) % 8))
-    beside = device(1 - x, z)
-    barrier = pltpu.get_barrier_semaphore()
-    for target in (*ring, beside):
-        pl.semaphore_signal(barrier, inc=1, device_id=target, device_id_type=MESH)
-    for copy in planes_in:
-        copy.wait()
 
     def term(x_to, z_to, store):
-        row = (x_to * 8 + z_to) * (2 * planes)
+        row = x_to * 8 + z_to
 
         def block(part, carry):
             rows = pl.ds(pl.multiple_of(part * 8, 8), 8)
-            total = cas[row] * own[0, rows, :]
+            total = cas[row, 0] * own[0, rows, :]
             for k in range(1, planes):
-                total += cas[row + k] * own[k, rows, :]
+                total += cas[row, k] * own[k, rows, :]
             for k in range(planes):
-                total += cas[row + planes + k] * other[k, rows, :]
+                total += cas[row, planes + k] * other[k, rows, :]
             store(rows, total)
             return carry
 
@@ -561,26 +573,20 @@
             flops=units * 2 * face**3, bytes_accessed=size * 4 * face**2, transcendentals=0
         )
 
-    here = lax.axis_index("gz")
     other_sources = swapped(sources, "gz")
-    o_33, o_31, near_gain, inv, through = pl.pallas_call(
+    cas, o_33, o_31, near_gain, inv, through = pl.pallas_call(
         near_kernel,
-        out_shape=[square] * 5,
-        in_specs=[ANY],
-        out_specs=[ANY] * 5,
+        out_shape=[jax.ShapeDtypeStruct((mode_ids.shape[0] // 2, 128), F32)] + [square] * 5,
+        in_specs=[pl.BlockSpec(memory_space=pltpu.SMEM), ANY],
+        out_specs=vmem_specs(1) + [ANY] * 5,
         scratch_shapes=[full] * 9
         + [left, left, left, right, right, short, short, full, pltpu.SemaphoreType.DMA((11,))],
         compiler_params=params,
         cost_estimate=cost(27, 11),
         name="level_one_near",
-    )(leaf_maps)
+    )(mode_ids, leaf_maps)
     y_33 = swapped(o_33, "box")
     y_32 = swapped(o_31, "box")
-    core = here % 2
-    modes = lax.dynamic_slice(mode_ids.reshape(-1, 2), (0, core), (16, 1)).reshape(16)
-    lanes = jnp.arange(planes, dtype=jnp.int32)
-    z_index = jnp.concatenate([here * planes + lanes, (here + 1 - 2 * core) * planes + lanes])
-    cas = cas_table(modes, z_index, NZ).reshape(-1)
     line = (boxes * rhs, points)
     pair = pltpu.VMEM((2 * face, face), BF16)
     o_11, o_13, near_data, far_data = pl.pallas_call(
@@ -619,9 +625,9 @@
     out, gain = pl.pallas_call(
         top_kernel,
         out_shape=[jax.ShapeDtypeStruct((face, points), F32), square],
-        in_specs=[ANY] * 5,
+        in_specs=vmem_specs(2) + [ANY] * 3,
         out_specs=[ANY] * 2,
-        scratch_shapes=[full] * 7
+        scratch_shapes=[full] * 5
         + [left, left, right, right, short, short, full, pltpu.SemaphoreType.DMA((8,))],
         compiler_params=pltpu.CompilerParams(vmem_limit_bytes=LESS_VMEM),
         cost_estimate=cost(22, 8),

time: 105 us -> 102 us (0.971)
  the two profiles are of different devices: /device:TPU:8 before, /device:TPU:250 now
where the time goes in v5:
time: 102 us
  Pallas kernels  96.8 us (95%)
  starting transfers between devices  4.37 us (4%)
    pallas_call x1, Pallas kernels, local(): pl.pallas_call(sums_kernel, out_shape=[square, square, rows, rows], in_sp...  51.1 us
    pallas_call x1, Pallas kernels, local(): pl.pallas_call(top_kernel, out_shape=[jax.ShapeDtypeStruct((face, points)...  29.6 us
    pallas_call x1, Pallas kernels, local(): pl.pallas_call(near_kernel, out_shape=[jax.ShapeDtypeStruct((mode_ids.sha...  13.3 us
    ppermute x4, starting transfers between devices, swapped(): return lax.ppermute(block, axis, route)  4.37 us
    pallas_call x1, Pallas kernels, local(): pl.pallas_call(last_kernel, out_shape=[jax.ShapeDtypeStruct((face, points...  2.81 us
  transfers between devices with their start and end apart: 4, of which 0 were waited for; matrix products, arithmetic and copies ran while one was open for 0% of the time, Pallas kernels for 92%

profile of v5, /device:TPU:250, one launch (start us, length us, event | category | flops | bytes accessed | tf_op | source)
XLA Modules:
  0.0 102.1 jit_solution(6021666833454448051)
XLA Ops:
  0.6 0.1 collective-permute-start.2
  0.7 13.3 %level_one_near.1 = (f32[16,128]{1,0:T(8,128)}, f32[512,512]{1,0:T(8,128)}, f32[512,512]{1,0:T(8,128)}, f32[512,512]{1,0:T(8,128)}, f32[512,512]{1,0:T(8,128)}, /*index=5*/f32[512,512]{1,0:T(8,128)}) custom-call(s32[32]{0:T(128)} %mode_ids.1, f32[1,2,1024,1024]{3,2,1,0:T(8,128)} %maps.3), custom_call_target="tpu_custom_call" | custom-call | flops 7247757312 | bytes 11534336 | tf_op jit(solution)/shard_map/level_one_near/pallas_call | solution.py:577
  14.0 0.8 collective-permute-start.1
  14.8 1.3 %collective-permute-start = (f32[512,512]{1,0:T(8,128)}, f32[512,512]{1,0:T(8,128)S(1)}, u32[]{:S(2)}, u32[]{:S(2)}) collective-permute-start(f32[512,512]{1,0:T(8,128)} %get-tuple-element.16.o_31_in), channel_id=1, source_target_pairs={{0,1},{1,0},{2,3},{3,2},{4,5},{5,4},{6,7},{7,6},{8,9},{9,8},{10,11... | collective-permute-start | bytes 3145736 | tf_op jit(solution)/shard_map/ppermute | solution.py:24
  16.1 0.0 collective-permute-done.2
  16.1 0.0 copy-start.2
  16.1 51.1 %hartley_sums.1 = (f32[512,512]{1,0:T(8,128)}, f32[512,512]{1,0:T(8,128)}, f32[16,512]{1,0:T(8,128)}, f32[16,512]{1,0:T(8,128)}) custom-call(f32[16,128]{1,0:T(8,128)} %get-tuple-element.18.cas, f32[16,32,1024]{2,1,0:T(8,128)} %bitcast.5, f32[16,32,1024]{2,1,0:T(8,128)} %bitcast.1.other_in, f32[1,2,1024,1024]{3,2,1,0:T(8,128)} %maps.3, ...), custom_call_target="tpu_custom_call" | custom-call | flops 26843545600 | bytes 5242880 | tf_op jit(solution)/shard_map/hartley_sums/pallas_call | solution.py:592
  67.2 2.2 %collective-permute-start.3 = (f32[16,512]{1,0:T(8,128)}, f32[16,512]{1,0:T(8,128)S(1)}, u32[]{:S(2)}, u32[]{:S(2)}) collective-permute-start(f32[16,512]{1,0:T(8,128)} %get-tuple-element.25.near_data), channel_id=1, source_target_pairs={{0,1},{1,0},{2,3},{3,2},{4,5},{5,4},{6,7},{7,6},{8,9},{9,8},{10,11... | collective-permute-start | bytes 98312 | tf_op jit(solution)/shard_map/ppermute | solution.py:24
  69.4 0.0 collective-permute-done.1.y_33
  69.4 0.0 copy-done.2
  69.4 0.0 copy-start
  69.4 0.0 copy-start.1
  69.4 29.6 %level_two_gain.1 = (f32[512,1024]{1,0:T(8,128)}, f32[512,512]{1,0:T(8,128)S(1)}) custom-call(f32[512,512]{1,0:T(8,128)S(1)} %collective-permute-done.1.y_33, f32[512,512]{1,0:T(8,128)S(1)} %copy-done.2, f32[512,512]{1,0:T(8,128)} %get-tuple-element.16.o_31_in, f32[512,512]{1,0:T(8,128)} %get-tuple-element.22.o_13_in, f32[512,512]{1,0:T(8,128)} %get-tuple-element.23.o_11_in), custom_call_target="tpu_custom_call" | custom-call | flops 5905580032 | bytes 8388608 | tf_op jit(solution)/shard_map/level_two_gain/pallas_call | solution.py:625
  99.1 0.0 collective-permute-done.y_32
  99.1 0.0 collective-permute-done.3.other_data
  99.1 0.0 copy-done
  99.1 0.0 copy-done.1
  99.1 2.8 %level_two_rows.1 = (f32[512,1024]{1,0:T(8,128)}, f32[16,512]{1,0:T(8,128)}) custom-call(f32[512,512]{1,0:T(8,128)S(1)} %collective-permute-done.y_32, f32[512,512]{1,0:T(8,128)S(1)} %get-tuple-element.24.gain, f32[512,512]{1,0:T(8,128)S(1)} %collective-permute-done.1.y_33, f32[16,512]{1,0:T(8,128)S(1)} %copy-done, ...), custom_call_target="tpu_custom_call", output_to_operand_aliasing={{0}: (6, {})} | custom-call | flops 1073741824 | bytes 5242880 | tf_op jit(solution)/shard_map/level_two_rows/pallas_call | solution.py:636
Async XLA Ops:
  0.6 15.5 %collective-permute-start.2 = (f32[16,2,16,1024]{3,2,1,0:T(8,128)}, f32[16,2,16,1024]{3,2,1,0:T(8,128)}, u32[]{:S(2)}, u32[]{:S(2)}) collective-permute-start(f32[16,2,16,1024]{3,2,1,0:T(8,128)} %param.3), channel_id=1, source_target_pairs={{0,8},{8,0},{16,24},{24,16},{32,40},{40,32},{48,56},{56,48},{64,72... | collective-permute-start | bytes 6291464 | tf_op jit(solution)/shard_map/ppermute | solution.py:24
  14.0 55.4 %collective-permute-start.1 = (f32[512,512]{1,0:T(8,128)}, f32[512,512]{1,0:T(8,128)S(1)}, u32[]{:S(2)}, u32[]{:S(2)}) collective-permute-start(f32[512,512]{1,0:T(8,128)} %get-tuple-element.17.o_33), channel_id=1, source_target_pairs={{0,1},{1,0},{2,3},{3,2},{4,5},{5,4},{6,7},{7,6},{8,9},{9,8},{10,11... | collective-permute-start | bytes 3145736 | tf_op jit(solution)/shard_map/ppermute | solution.py:24
  14.8 84.2 %collective-permute-start = (f32[512,512]{1,0:T(8,128)}, f32[512,512]{1,0:T(8,128)S(1)}, u32[]{:S(2)}, u32[]{:S(2)}) collective-permute-start(f32[512,512]{1,0:T(8,128)} %get-tuple-element.16.o_31_in), channel_id=1, source_target_pairs={{0,1},{1,0},{2,3},{3,2},{4,5},{5,4},{6,7},{7,6},{8,9},{9,8},{10,11... | collective-permute-start | bytes 3145736 | tf_op jit(solution)/shard_map/ppermute | solution.py:24
  16.1 53.3 %copy-start.2 = (f32[512,512]{1,0:T(8,128)S(1)}, f32[512,512]{1,0:T(8,128)}, u32[]{:S(2)}) copy-start(f32[512,512]{1,0:T(8,128)} %get-tuple-element.17.o_33) | copy-start | bytes 3145732
  67.2 31.8 %collective-permute-start.3 = (f32[16,512]{1,0:T(8,128)}, f32[16,512]{1,0:T(8,128)S(1)}, u32[]{:S(2)}, u32[]{:S(2)}) collective-permute-start(f32[16,512]{1,0:T(8,128)} %get-tuple-element.25.near_data), channel_id=1, source_target_pairs={{0,1},{1,0},{2,3},{3,2},{4,5},{5,4},{6,7},{7,6},{8,9},{9,8},{10,11... | collective-permute-start | bytes 98312 | tf_op jit(solution)/shard_map/ppermute | solution.py:24
  69.4 29.7 %copy-start = (f32[16,512]{1,0:T(8,128)S(1)}, f32[16,512]{1,0:T(8,128)}, u32[]{:S(2)}) copy-start(f32[16,512]{1,0:T(8,128)} %get-tuple-element.25.near_data) | copy-start | bytes 98308
  69.4 29.7 %copy-start.1 = (f32[16,512]{1,0:T(8,128)S(1)}, f32[16,512]{1,0:T(8,128)}, u32[]{:S(2)}) copy-start(f32[16,512]{1,0:T(8,128)} %get-tuple-element.26.far_data) | copy-start | bytes 98308
